TPU v7x, 32 devices: a whole 2x2x4 slice. The times are simulated.
32 devices in a mesh: grp: 2 (over x), kern: 2 (over core), row: 8 (over z, y).
Axes of the slice: x: 2, y: 2, z: 4, core: 2. Of those that a mesh axis runs over, the one named last changes fastest.
Arguments:
- mask_levels: float32 [4096, 2048], P(('grp', 'row'), 'kern'), parts along dimension 0, may hold values from -6 to 6
- target_image: float32 [4096, 2048], P(('grp', 'row'), 'kern'), parts along dimension 0, may hold values from 0 to 1
- diffusion_index: int32 [128, 64], P(('grp', 'row'), 'kern'), parts along dimension 0, may hold values from 0 to 7
- diffusion_table: float32 [8], replicated, may hold values from 0.04 to 0.24
- kernel_weights: float32 [16], P('kern'), may hold values from 0.02 to 0.2
- kernel_spectra: float32 [2, 16, 256, 256], P(None, 'kern'), may hold values from -5 to 5
Outputs:
- gradient: float32 [4096, 2048], P(('grp', 'row'), 'kern'), parts along dimension 0
- resist: float32 [4096, 2048], P(('grp', 'row'), 'kern'), parts along dimension 0
There are 2 independent parts, one for each index of `grp`. A program takes and returns all parts, laid end to end along the dimension named above; an argument that names none is the same for every part. Nothing has to cross between parts.
All inputs are finite; a program needn't handle non-finite values.
Results may differ from a plain program's by a relative error of at most 0.0003.
Values sent between devices are 32-bit elements; how exact they have to be, the bound alone decides.
A program may use at most 128 MiB of HBM per device.

v0:
```python
import jax
import jax.numpy as jnp
from jax import lax
from jax.sharding import PartitionSpec as P

PIXELS = 2048
BAND = 256
BLOCK = 32
LEVELS = 8
STEPS = 4


steepness = 8.0
threshold = 0.5
highest = lax.Precision.HIGHEST


def padded(shard, sides, width):
    for axis, dim in sides:
        size, length = (lax.axis_size(axis), shard.shape[dim])
        up = [(i, (i + 1) % size) for i in range(size - 1)]
        down = [(j, i) for i, j in up]
        last = lax.slice_in_dim(shard, length - width, length, axis=dim)
        initial = lax.slice_in_dim(shard, 0, width, axis=dim)
        before = lax.ppermute(last, axis, up)
        after = lax.ppermute(initial, axis, down)
        shard = jnp.concatenate([before, shard, after], axis=dim)
    return shard


def matmul(left_side, right_side):
    return jnp.dot(left_side, right_side, precision=highest, preferred_element_type=jnp.float32)


def inner_rows(left_side, right_side):
    return lax.dot_general(
        left_side,
        right_side,
        (((0,), (0,)), ((), ())),
        precision=highest,
        preferred_element_type=jnp.float32,
    )


def dft_tables(positions):
    frequency = jnp.arange(BAND, dtype=jnp.int32) - BAND // 2
    product = jnp.mod(frequency[:, None] * positions[None, :], PIXELS)
    angles = 2.0 * jnp.pi / PIXELS * product.astype(jnp.float32)
    return (jnp.cos(angles), jnp.sin(angles))


def forward_table(cosines, sine_part):
    upper_rows = jnp.concatenate([cosines, sine_part], 1)
    lower_rows = jnp.concatenate([-sine_part, cosines], 1)
    return jnp.concatenate([upper_rows, lower_rows], 0)


def diffuse_inner(values, root_field):
    centre = values[1:-1, 1:-1]
    running = root_field[:-2, 1:-1] * (values[:-2, 1:-1] - centre)
    running = running + root_field[2:, 1:-1] * (values[2:, 1:-1] - centre)
    running = running + root_field[1:-1, :-2] * (values[1:-1, :-2] - centre)
    running = running + root_field[1:-1, 2:] * (values[1:-1, 2:] - centre)
    return centre + root_field[1:-1, 1:-1] * running


def deep_steps(values, root_rim):
    for iteration in range(STEPS):
        root_now = root_rim[
            iteration : root_rim.shape[0] - iteration, iteration : root_rim.shape[1] - iteration
        ]
        values = diffuse_inner(values, root_now)
    return values


def adjoint_rows(sens_piece, local_start, fields, table_out, weights):
    span_count = sens_piece.shape[1]
    total_cols = table_out.shape[1] // 2
    local_start = jnp.asarray(local_start)
    table_piece = jnp.concatenate(
        [
            lax.dynamic_slice_in_dim(table_out, local_start, span_count, 1),
            lax.dynamic_slice_in_dim(table_out, total_cols, span_count, 1),
        ],
        1,
    )
    field_re = lax.dynamic_slice_in_dim(fields, local_start, span_count, 2)
    field_im = lax.dynamic_slice_in_dim(fields, total_cols, span_count, 2)
    scaled = 2.0 * weights[:, None, None] * sens_piece[None, :, :]
    stacked = jnp.concatenate([scaled * field_re, scaled * field_im], 2)
    return jnp.einsum(
        "kij,pj->kip", stacked, table_piece, precision=highest, preferred_element_type=jnp.float32
    )


def body(
    mask_levels, target_image, diffusion_index, diffusion_table, kernel_weights, kernel_spectra
):
    height, breadth = mask_levels.shape
    row_start = lax.axis_index("row") * height
    col_start = lax.axis_index("kern") * breadth
    cos_rows, sin_rows = dft_tables(row_start + jnp.arange(height, dtype=jnp.int32))
    cos_cols, sin_cols = dft_tables(col_start + jnp.arange(breadth, dtype=jnp.int32))
    transmit = jnp.tanh(mask_levels)
    halfway = lax.dot_general(
        transmit,
        jnp.concatenate([cos_cols, -sin_cols], 0),
        (((1,), (1,)), ((), ())),
        precision=highest,
        preferred_element_type=jnp.float32,
    )
    half_re = halfway[:, :BAND]
    half_im = halfway[:, BAND:]
    spec_re = (matmul(cos_rows, half_re) + matmul(sin_rows, half_im)) / PIXELS
    spec_im = (matmul(cos_rows, half_im) - matmul(sin_rows, half_re)) / PIXELS
    spec_re, spec_im = lax.psum((spec_re, spec_im), ("kern", "row"))
    field_cos, field_sin = dft_tables(jnp.arange(PIXELS, dtype=jnp.int32))
    pupil_re = kernel_spectra[0]
    pupil_im = kernel_spectra[1]
    grid_re = pupil_re * spec_re - pupil_im * spec_im
    grid_im = pupil_re * spec_im + pupil_im * spec_re
    left_re = jnp.einsum(
        "pi,kpq->kiq", cos_rows, grid_re, precision=highest, preferred_element_type=jnp.float32
    ) - jnp.einsum(
        "pi,kpq->kiq", sin_rows, grid_im, precision=highest, preferred_element_type=jnp.float32
    )
    left_im = jnp.einsum(
        "pi,kpq->kiq", cos_rows, grid_im, precision=highest, preferred_element_type=jnp.float32
    ) + jnp.einsum(
        "pi,kpq->kiq", sin_rows, grid_re, precision=highest, preferred_element_type=jnp.float32
    )
    left_half = jnp.concatenate([left_re, left_im], 2) / BAND
    table_out = forward_table(field_cos, field_sin)
    fields = jnp.einsum(
        "kip,pj->kij", left_half, table_out, precision=highest, preferred_element_type=jnp.float32
    )
    span_count = field_cos.shape[1]
    power_sum = jnp.einsum(
        "k,kij->ij",
        kernel_weights,
        fields[:, :, :span_count] ** 2 + fields[:, :, span_count:] ** 2,
        precision=highest,
        preferred_element_type=jnp.float32,
    )
    intensity = lax.psum_scatter(power_sum, "kern", scatter_dimension=1, tiled=True)
    levels_onehot = (diffusion_index[:, :, None] == jnp.arange(LEVELS, dtype=jnp.int32)).astype(
        jnp.float32
    )
    block_root = jnp.dot(levels_onehot, jnp.sqrt(diffusion_table), precision=highest)
    block_rows, block_cols = block_root.shape
    root_tile = jnp.broadcast_to(
        block_root[:, None, :, None], (block_rows, BLOCK, block_cols, BLOCK)
    )
    root_tile = root_tile.reshape(height, breadth)
    extended = padded(jnp.stack([intensity, root_tile]), (("kern", 2), ("row", 1)), STEPS)
    root_rim = extended[1]
    acid_level = deep_steps(extended[0], root_rim)
    resist = jax.nn.sigmoid(steepness * (acid_level - threshold))
    sensitivity = 2.0 * steepness * resist * (1.0 - resist) * (resist - target_image)
    sens_rim = padded(sensitivity, (("kern", 1), ("row", 0)), STEPS)
    sensitivity = deep_steps(sens_rim, root_rim)
    accumulated = adjoint_rows(
        lax.all_gather(sensitivity, "kern", axis=1, tiled=True),
        jnp.int32(0),
        fields,
        table_out,
        kernel_weights,
    )
    accum_re = accumulated[:, :, :BAND]
    accum_im = -accumulated[:, :, BAND:]
    inner_re = jnp.einsum(
        "pi,kiq->kpq", cos_rows, accum_re, precision=highest, preferred_element_type=jnp.float32
    ) - jnp.einsum(
        "pi,kiq->kpq", sin_rows, accum_im, precision=highest, preferred_element_type=jnp.float32
    )
    inner_im = jnp.einsum(
        "pi,kiq->kpq", cos_rows, accum_im, precision=highest, preferred_element_type=jnp.float32
    ) + jnp.einsum(
        "pi,kiq->kpq", sin_rows, accum_re, precision=highest, preferred_element_type=jnp.float32
    )
    back_re = jnp.sum(pupil_re * inner_re - pupil_im * inner_im, axis=0)
    back_im = jnp.sum(pupil_re * inner_im + pupil_im * inner_re, axis=0)
    back_re, back_im = lax.psum((back_re, back_im), ("kern", "row"))
    mixed_re = inner_rows(cos_rows, back_re) + inner_rows(sin_rows, back_im)
    mixed_im = inner_rows(cos_rows, back_im) - inner_rows(sin_rows, back_re)
    grad_trans = (matmul(mixed_re, cos_cols) + matmul(mixed_im, sin_cols)) / (PIXELS * BAND)
    gradient = grad_trans * (1.0 - transmit * transmit)
    return (gradient, resist)


def solution(mesh):
    return jax.shard_map(
        body,
        mesh=mesh,
        in_specs=(
            P(("grp", "row"), "kern"),
            P(("grp", "row"), "kern"),
            P(("grp", "row"), "kern"),
            P(),
            P("kern"),
            P(None, "kern", None, None),
        ),
        out_specs=(P(("grp", "row"), "kern"), P(("grp", "row"), "kern")),
        check_vma=False,
    )
```

profile of v0, /device:TPU:0, one launch (start us, length us, event | category | flops | bytes accessed | tf_op | source)
XLA Modules:
  0.0 541.7 jit_solution(16263493505943986283)
XLA Ops:
  7.3 4.2 fusion.127
  11.4 1.9 fusion.36
  13.3 1.4 fusion.151
  14.7 1.4 fusion.155
  16.1 2.1 fusion.93
  18.2 2.1 fusion.94
  20.4 10.4 %fusion.122 = (f32[256,2048]{1,0:T(8,128)}, f32[256,2048]{1,0:T(8,128)}, f32[256,2048]{1,0:T(8,128)}) fusion(s32[256]{0:T(256)S(1)} %get-tuple-element.30), kind=kLoop, calls=%fused_computation.192 | loop fusion | flops 7864320 | bytes 6292480 | tf_op jit(solution)/shard_map/sin | solution.py:49
  30.8 2.5 fusion.257
  33.3 1.9 copy.31
  35.2 3.3 copy.32
  38.5 74.8 %all-reduce.7.cloned.1.call-done = (f32[256,256]{1,0:T(8,128)}, f32[256,256]{1,0:T(8,128)}) async-done(((f32[256,256]{1,0:T(8,128)}, f32[256,256]{1,0:T(8,128)}), (f32[256,256]{1,0:T(8,128)}, f32[256,256]{1,0:T(8,128)})) %all-reduce.7.cloned.1.call-update) | async-done | bytes 524304 | tf_op jit(solution)/shard_map/psum | solution.py:116
  113.3 1.1 copy.19
  114.4 1.1 copy.17
  115.5 5.0 fusion.130
  120.5 3.4 fusion.134
  123.9 3.4 add_bitcast_fusion
  127.4 3.4 subtract_bitcast_fusion
  130.9 62.2 %fusion.6 = f32[8,256,4096]{2,1,0:T(8,128)} fusion(f32[256,2048]{1,0:T(8,128)S(1)} %copy-done.8, f32[256,2048]{1,0:T(8,128)S(1)} %copy-done.7, f32[256,2048]{1,0:T(8,128)S(1)} %copy-done.6, f32[8,256,256]{2,1,0:T(8,128)S(1)} %add_bitcast_fusion, f32[8,256,256]{2,1,0:T(8,128)S(1)} %subtract_bitcast_fusion), kind=kOutput, calls=%fused_computation.10 | convolution fusion | flops 51547996160 | bytes 44040192 | tf_op jit(solution)/shard_map/kip,pj->kij/dot_general | solution.py:134
  193.1 11.7 %multiply_add_fusion = f32[8,256,2048]{2,1,0:T(8,128)S(1)} fusion(f32[8,256,4096]{2,1,0:T(8,128)} %fusion.6), kind=kLoop, calls=%fused_computation.8 | loop fusion | flops 12582912 | bytes 50331648 | tf_op jit(solution)/shard_map/add | solution.py:141
  204.9 21.8 %fusion.4 = f32[1,256,2048]{2,0,1:T(1,128)} fusion(f32[8,256,2048]{2,1,0:T(8,128)S(1)} %multiply_add_fusion, f32[8]{0:T(128)S(1)} %copy-done.12), kind=kOutput, calls=%fused_computation.6 | convolution fusion | flops 50331648 | bytes 18874400 | tf_op jit(solution)/shard_map/k,kij->ij/dot_general | solution.py:138
  226.6 3.8 copy.36
  231.5 2.7 broadcast_in_dim.2
  234.2 4.0 stack_reshape.3
  238.2 2.5 reduce-scatter.2.cloned.1.call-done
  240.7 1.2 fusion.142
  241.9 1.3 collective-permute-start.1
  243.2 3.8 collective-permute-start
  247.0 1.6 pad_maximum_fusion
  248.6 4.3 concatenate.36
  252.9 0.9 fusion.258
  253.8 3.7 collective-permute-start.2
  257.5 1.5 collective-permute-start.3
  259.1 4.2 collective-permute-done.3
  263.3 1.9 pad_maximum_fusion.1
  265.3 2.6 fusion.87
  268.0 3.0 fusion.78
  271.0 3.0 fusion.69
  274.1 3.7 subtract_multiply_fusion
  277.7 1.0 copy-done.3
  278.8 1.3 collective-permute-start.5
  280.1 3.9 collective-permute-start.4
  284.4 2.4 concatenate.38
  287.6 4.3 collective-permute-start.6
  291.9 1.3 collective-permute-start.7
  293.4 4.2 collective-permute-done.7
  297.6 1.4 pad_maximum_fusion.2
  299.0 2.6 fusion.60
  301.6 3.0 fusion.51
  304.6 3.0 fusion.42
  307.7 3.6 fusion.101
  311.8 10.2 %all-gather.2.cloned.1.call-done = f32[256,2048]{1,0:T(8,128)} async-done(((f32[256,1024]{1,0:T(8,128)}), f32[256,2048]{1,0:T(8,128)}) %all-gather.2.cloned.1.call-update) | async-done | bytes 2097168 | tf_op jit(solution)/shard_map/all_gather | solution.py:163
  322.0 17.8 %multiply_multiply_fusion.1 = (f32[8,256,2048]{2,1,0:T(8,128)S(1)}, f32[8,256,2048]{2,1,0:T(8,128)}) fusion(f32[8,256,4096]{2,1,0:T(8,128)} %fusion.6, f32[256,2048]{1,0:T(8,128)} %all-gather.2.cloned.1.call-done, f32[8]{0:T(128)S(1)} %broadcast_multiply_fusion), kind=kLoop, calls=%fused_computation.5 | loop fusion | flops 12582912 | bytes 69206048 | tf_op jit(solution)/shard_map/mul | solution.py:90
  339.8 63.1 %fusion = f32[8,256,512]{2,1,0:T(8,128)} fusion(f32[8,256,2048]{2,1,0:T(8,128)} %get-tuple-element.11, f32[8,256,2048]{2,1,0:T(8,128)S(1)} %get-tuple-element.10, f32[256,2048]{1,0:T(8,128)} %get-tuple-element.28, f32[256,2048]{1,0:T(8,128)} %get-tuple-element.27, f32[256,2048]{1,0:T(8,128)} %get-tuple-element.26), kind=kOutput, calls=%fused_computation | convolution fusion | flops 51554287616 | bytes 44040192 | tf_op jit(solution)/shard_map/kij,pj->kip/dot_general | solution.py:91
  402.9 6.0 %fusion.26 = f32[8,256,256]{2,1,0:T(8,128)S(1)} fusion(f32[8,256,512]{2,1,0:T(8,128)} %fusion, s32[256]{0:T(256)S(1)} %get-tuple-element.29, s32[256]{0:T(256)S(1)} %get-tuple-element.30), kind=kOutput, calls=%fused_computation.52 | convolution fusion | flops 1611530240 | bytes 4196352 | tf_op jit(solution)/shard_map/pi,kiq->kpq/dot_general | solution.py:178
  409.0 4.4 fusion.28
  413.4 4.6 fusion.32
  418.1 5.6 %fusion.19 = (f32[256,256]{0,1:T(8,128)}, f32[256,256]{0,1:T(8,128)}) fusion(f32[8,256,256]{2,1,0:T(8,128)S(1)} %fusion.32, f32[1,8,256,256]{2,3,1,0:T(8,128)S(1)} %copy-done.1, f32[1,8,256,256]{2,3,1,0:T(8,128)S(1)} %copy.31, f32[8,256,256]{2,1,0:T(8,128)S(1)} %fusion.26, s32[256]{0:T(256)S(1)} %get-tuple-element.29, s32[256]{0:T(256)S(1)} %get-tuple-element.30, ...), kind=kOutput, calls=%fused_computation.36 | convolution fusion | flops 1616642048 | bytes 11012096 | tf_op jit(solution)/shard_map/pi,kiq->kpq/dot_general | solution.py:176
  423.7 91.4 %all-reduce.5.cloned.1.call-done = (f32[256,256]{0,1:T(8,128)}, f32[256,256]{0,1:T(8,128)}) async-done(((f32[256,256]{0,1:T(8,128)}, f32[256,256]{0,1:T(8,128)}), (f32[256,256]{0,1:T(8,128)}, f32[256,256]{0,1:T(8,128)})) %all-reduce.5.cloned.1.call-update) | async-done | bytes 524304 | tf_op jit(solution)/shard_map/psum | solution.py:183
  515.1 2.6 fusion.162
  517.7 2.5 fusion.164
  520.3 1.6 convolution_add_fusion.1
  521.9 1.8 convolution_subtract_fusion
  523.7 4.9 fusion.136
  528.6 6.0 %fusion.35 = f32[256,1024]{1,0:T(8,128)} fusion(f32[256,1024]{1,0:T(8,128)S(1)} %fusion.136, f32[256,256]{1,0:T(8,128)S(1)} %convolution_subtract_fusion, f32[256,1024]{1,0:T(8,128)S(1)} %copy-done.10, s32[1024]{0:T(1024)S(1)} %iota_add_fusion, s32[256]{0:T(256)S(1)} %get-tuple-element.30), kind=kOutput, calls=%fused_computation.67 | convolution fusion | flops 810287104 | bytes 3412992 | tf_op jit(solution)/shard_map/dot_general | solution.py:32
  (54 shorter events, 3.5 us)
Async XLA Ops:
  7.2 4.3 copy-start.9
  7.2 106.1 %all-reduce.7.cloned.1.call-start = ((), (), s32[]{:S(2)}) async-start(), calls=%async_computation.4 | async-start | bytes 1048576 | tf_op jit(solution)/shard_map/psum | solution.py:116
  20.4 220.3 %reduce-scatter.2.cloned.1.call-start = ((), (), s32[]{:S(2)}) async-start(), calls=%async_computation.1 | async-start | bytes 3145728 | tf_op jit(solution)/shard_map/reduce_scatter | solution.py:145
  20.4 10.4 %copy-start.4 = (f32[2,8,256,256]{3,2,1,0:T(8,128)S(1)}, f32[2,8,256,256]{3,2,1,0:T(8,128)}, u32[]{:S(2)}) copy-start(f32[2,8,256,256]{3,2,1,0:T(8,128)} %param.11) | copy-start | bytes 12582916
  115.5 5.0 copy-start
  127.4 3.5 copy-start.6
  127.4 3.5 copy-start.7
  127.4 3.5 copy-start.8
  193.1 11.8 %copy-start.12 = (f32[8]{0:T(128)S(1)}, f32[8]{0:T(128)}, u32[]{:S(2)}) copy-start(f32[8]{0:T(128)} %param.10) | copy-start | bytes 100
  230.4 0.7 copy-start.15
  230.4 0.7 copy-start.16
  230.4 91.6 %all-gather.2.cloned.1.call-start = ((), (), s32[]{:S(2)}) async-start(), calls=%async_computation.2 | async-start | bytes 3145728 | tf_op jit(solution)/shard_map/all_gather | solution.py:163
  240.7 6.3 %copy-start.5 = (f32[256,1024]{1,0:T(8,128)S(1)}, f32[256,1024]{1,0:T(8,128)}, u32[]{:S(2)}) copy-start(f32[256,1024]{1,0:T(8,128)} %reduce-scatter.2.cloned.1.call-done) | copy-start | bytes 3145732
  241.9 6.7 %collective-permute-start.1 = (f32[2,256,4]{2,1,0:T(8,128)S(1)}, f32[2,256,4]{2,1,0:T(8,128)S(1)}, u32[]{:S(2)}, u32[]{:S(2)}) collective-permute-start(f32[2,256,4]{2,1,0:T(8,128)S(1)} %get-tuple-element.18), channel_id=1, source_target_pairs={{8,0},{9,1},{10,2},{11,3},{12,4},{13,5},{14,6},{15,7},{24,16},{25,... | collective-permute-start | bytes 24584 | tf_op jit(solution)/shard_map/ppermute | solution.py:26
  243.2 5.4 collective-permute-start
  253.8 5.3 collective-permute-start.2
  257.5 5.9 %collective-permute-start.3 = (f32[2,4,1032]{2,1,0:T(4,128)S(1)}, f32[2,4,1032]{2,1,0:T(4,128)S(1)}, u32[]{:S(2)}, u32[]{:S(2)}) collective-permute-start(f32[2,4,1032]{2,1,0:T(4,128)S(1)} %get-tuple-element.17), channel_id=1, source_target_pairs={{1,0},{2,1},{3,2},{4,3},{5,4},{6,5},{7,6},{9,8},{10,9},{11,10},{12... | collective-permute-start | bytes 99080 | tf_op jit(solution)/shard_map/ppermute | solution.py:26
  271.0 3.1 copy-start.11
  277.7 1.0 copy-start.3
  278.8 5.2 collective-permute-start.5
  280.1 4.4 collective-permute-start.4
  287.6 5.8 %collective-permute-start.6 = (f32[4,1032]{1,0:T(4,128)S(1)}, f32[4,1032]{1,0:T(4,128)S(1)}, u32[]{:S(2)}, u32[]{:S(2)}) collective-permute-start(f32[4,1032]{1,0:T(4,128)S(1)} %get-tuple-element.20), channel_id=1, source_target_pairs={{0,1},{1,2},{2,3},{3,4},{4,5},{5,6},{6,7},{8,9},{9,10},{10,11},{11... | collective-permute-start | bytes 49544 | tf_op jit(solution)/shard_map/ppermute | solution.py:25
  291.9 5.7 %collective-permute-start.7 = (f32[4,1032]{1,0:T(4,128)S(1)}, f32[4,1032]{1,0:T(4,128)S(1)}, u32[]{:S(2)}, u32[]{:S(2)}) collective-permute-start(f32[4,1032]{1,0:T(4,128)S(1)} %get-tuple-element.21), channel_id=1, source_target_pairs={{1,0},{2,1},{3,2},{4,3},{5,4},{6,5},{7,6},{9,8},{10,9},{11,10},{12... | collective-permute-start | bytes 49544 | tf_op jit(solution)/shard_map/ppermute | solution.py:26
  311.3 203.8 %all-reduce.5.cloned.1.call-start = ((), (), s32[]{:S(2)}) async-start(), calls=%async_computation.3 | async-start | bytes 1048576 | tf_op jit(solution)/shard_map/psum | solution.py:183
  402.9 6.1 %copy-start.2 = (f32[8,256,512]{2,1,0:T(8,128)S(1)}, f32[8,256,512]{2,1,0:T(8,128)}, u32[]{:S(2)}) copy-start(f32[8,256,512]{2,1,0:T(8,128)} %fusion) | copy-start | bytes 12582916
  413.4 4.6 copy-start.1
  515.1 5.1 copy-start.14
  515.1 6.7 %copy-start.13 = (f32[256,256]{0,1:T(8,128)S(1)}, f32[256,256]{0,1:T(8,128)}, u32[]{:S(2)}) copy-start(f32[256,256]{0,1:T(8,128)} %get-tuple-element.4) | copy-start | bytes 786436
  523.7 4.9 copy-start.10
Sparse Core Ops, SparseCore 0:
  20.5 92.7 all-reduce.6
  230.6 10.1 reduce-scatter.1
  311.4 10.5 all-gather.1
  423.8 91.2 all-reduce.4
where the time goes:
time: 552 us; the launch traced here: 542 us
  matrix products  212 us (38%)
  waiting for transfers between devices  188 us (34%)
  other arithmetic  74.8 us (14%)
  local copies, waits for them, and re-layouts  30.6 us (6%)
  starting transfers between devices  21.5 us (4%)
  between operations  14.7 us (3%)
    psum x1, waiting for transfers between devices, body(): back_re, back_im = lax.psum((back_re, back_im), ('kern', 'row'))  91.4 us
    psum x1, waiting for transfers between devices, body(): spec_re, spec_im = lax.psum((spec_re, spec_im), ('kern', 'row'))  74.8 us
    dot_general x1, matrix products, adjoint_rows(): jnp.einsum('kij,pj->kip', stacked, table_piece, precision=highest, prefer...  63.1 us
    dot_general x1, matrix products, body(): jnp.einsum('kip,pj->kij', left_half, table_out, precision=highest, prefer...  62.2 us
    dot_general x1, matrix products, body(): jnp.einsum('k,kij->ij', kernel_weights, fields[:, :, :span_count] ** 2 +...  21.8 us
    add x7, other arithmetic, diffuse_inner(): return centre + root_field[1:-1, 1:-1] * running  21 us
    dot_general x6, matrix products, matmul(): jnp.dot(left_side, right_side, precision=highest, preferred_element_type=...  17.9 us
    mul x1, other arithmetic, adjoint_rows(): stacked = jnp.concatenate([scaled * field_re, scaled * field_im], 2)  17.8 us
  transfers between devices with their start and end apart: 12, of which 9 were waited for; matrix products, arithmetic and copies ran while one was open for 5% of the time, Pallas kernels for 0%

commit v1 on v0

v1 whole, which is shorter than its diff:
```python
import numpy as np
import jax
import jax.numpy as jnp
from jax import lax
from jax.sharding import PartitionSpec as P

PIXELS = 2048
BAND = 256
BLOCK = 32
STEPS = 4
HALF = BAND // 2
GRID = 2 * BAND
HALO = 2 * STEPS
LANES = 128
steepness = 8.0
threshold = 0.5
high = lax.Precision.HIGHEST


def mm(a, b):
    return jnp.dot(a, b, precision=high, preferred_element_type=jnp.float32)


def mm_ta(a, b):
    return lax.dot_general(a, b, (((0,), (0,)), ((), ())), precision=high, preferred_element_type=jnp.float32)


def mm_tb(a, b):
    return lax.dot_general(a, b, (((1,), (1,)), ((), ())), precision=high, preferred_element_type=jnp.float32)


def mask_table():
    n = np.arange(HALF)
    f = np.concatenate([n, -(n + 1)])
    angle = 2 * np.pi / PIXELS * ((f[:, None] * np.arange(PIXELS)[None, :]) % PIXELS)
    return np.cos(angle), np.sin(angle)


def half_table(positions):
    n = np.arange(HALF)
    angle = np.pi / PIXELS * (((2 * n + 1)[:, None] * positions[None, :]) % (2 * PIXELS))
    return np.concatenate([np.cos(angle), np.sin(angle)], 0)


def interpolation_table():
    d = np.arange(PIXELS)[:, None] - (PIXELS // GRID) * np.arange(GRID)[None, :]
    d = d % PIXELS
    safe = np.where(d == 0, 1, d)
    u = np.sin(2 * np.pi * ((BAND * safe) % PIXELS) / PIXELS) / (GRID * np.tan(np.pi * safe / PIXELS))
    return np.where(d == 0, 1.0, u)


def const(x):
    return jnp.asarray(x.astype(np.float32))


def fold(h):
    h = jnp.concatenate([h[..., HALF:, :], jnp.flip(h[..., :HALF, :], -2)], -2)
    return jnp.concatenate([h[..., HALF:], jnp.flip(h[..., :HALF], -1)], -1)


def diffuse(acid, root):
    up = jnp.roll(root, 1, 0) * (jnp.roll(acid, 1, 0) - acid)
    up = up + jnp.roll(root, -1, 0) * (jnp.roll(acid, -1, 0) - acid)
    up = up + jnp.roll(root, 1, 1) * (jnp.roll(acid, 1, 1) - acid)
    up = up + jnp.roll(root, -1, 1) * (jnp.roll(acid, -1, 1) - acid)
    return acid + root * up


def quads(g):
    a, b, c, d = g[..., :HALF, :HALF], g[..., :HALF, HALF:], g[..., HALF:, :HALF], g[..., HALF:, HALF:]
    return a + b + c + d, a + c - b - d, a + b - c - d, a - b - c + d


def join(a, b, c, d):
    return jnp.concatenate([jnp.concatenate([a, b], -1), jnp.concatenate([c, d], -1)], -2)


def body(mask_levels, target_image, diffusion_index, diffusion_table, kernel_weights, kernel_spectra):
    height, breadth = mask_levels.shape
    rows_n, cols_n = lax.axis_size("row"), lax.axis_size("kern")
    row, col = lax.axis_index("row"), lax.axis_index("kern")
    row_start, col_start = row * height, col * breadth
    tall, wide = height + 2 * HALO, breadth + LANES

    ct, st = mask_table()
    cut_rows = lambda t, s, n: lax.dynamic_slice_in_dim(t, s, n, 0)
    col_tab = cut_rows(const(np.concatenate([ct.T, st.T], 1)), col_start, breadth)
    row_tab = cut_rows(const(np.concatenate([ct.T, st.T], 1)), row_start, height)

    row_pos = np.concatenate([np.arange(rows_n * height), [0] * 0])
    base = half_table(np.arange(-HALO, PIXELS + HALO)).T
    r_mid = cut_rows(const(base), row_start, tall)
    r_tab = jnp.concatenate([r_mid[HALO:], r_mid[:HALO]], 0)
    t_tab = const(half_table(np.arange(GRID) * (PIXELS // GRID)))
    inter = interpolation_table()
    inter = np.concatenate([inter[-LANES // 2:], inter, inter[:LANES // 2]], 0)
    u_mid = cut_rows(const(inter), col_start, wide)
    u_tab = jnp.concatenate([u_mid[LANES // 2:], u_mid[:LANES // 2]], 0)

    transmit = jnp.tanh(mask_levels)
    halfway = mm(transmit, col_tab)
    prod = mm_ta(row_tab, halfway)
    scale = 1.0 / (PIXELS * BAND)
    s_re = (prod[:BAND, :BAND] - prod[BAND:, BAND:]) * scale
    s_im = -(prod[BAND:, :BAND] + prod[:BAND, BAND:]) * scale
    s_re, s_im = lax.psum((s_re, s_im), ("kern", "row"))

    hot = (diffusion_index[:, :, None] == jnp.arange(diffusion_table.shape[0], dtype=jnp.int32)).astype(jnp.float32)
    block_root = jnp.sum(hot * jnp.sqrt(diffusion_table), -1)
    br, bc = block_root.shape
    root = jnp.broadcast_to(block_root[:, None, :, None], (br, BLOCK, bc, BLOCK)).reshape(height, breadth)
    both = jnp.stack([target_image, root])
    up = [(i, (i + 1) % cols_n) for i in range(cols_n - 1)]
    dn = [(j, i) for i, j in up]
    right = lax.ppermute(both[:, :, : LANES // 2], "kern", dn)
    left = lax.ppermute(both[:, :, breadth - LANES // 2:], "kern", up)
    both = jnp.concatenate([both, right, left], 2)
    up = [(i, i + 1) for i in range(rows_n - 1)]
    dn = [(j, i) for i, j in up]
    below = lax.ppermute(both[:, :HALO], "row", dn)
    above = lax.ppermute(both[:, height - HALO:], "row", up)
    both = jnp.concatenate([both, below, above], 1)
    target, root = both[0], both[1]

    h = fold(kernel_spectra)
    h_re, h_im = h[0], h[1]
    g_re = h_re * s_re - h_im * s_im
    g_im = h_re * s_im + h_im * s_re
    ee_r, eo_r, oe_r, oo_r = quads(g_re)
    ee_i, eo_i, oe_i, oo_i = quads(g_im)
    m = jnp.stack([join(ee_r, -eo_i, -oe_i, -oo_r), join(ee_i, eo_r, oe_r, -oo_i)])
    left_part = jnp.einsum("ip,ckpq->ckiq", r_tab, m, precision=high, preferred_element_type=jnp.float32)
    fields = jnp.einsum("ckiq,qj->ckij", left_part, t_tab, precision=high, preferred_element_type=jnp.float32)
    power = jnp.sum(kernel_weights[:, None, None] * (fields[0] ** 2 + fields[1] ** 2), 0)
    power = lax.psum(power, "kern")
    acid = mm_tb(power, u_tab)
    for _ in range(STEPS):
        acid = diffuse(acid, root)
    resist = jax.nn.sigmoid(steepness * (acid - threshold))
    sens = 2.0 * steepness * resist * (1.0 - resist) * (resist - target)
    for _ in range(STEPS):
        sens = diffuse(sens, root)
    q_grid = mm(sens[:height, :breadth], u_tab[:breadth])
    q_grid = lax.psum(q_grid, "kern")
    d_field = (2.0 * kernel_weights)[:, None, None] * q_grid * fields[:, :, :height]
    d_left = jnp.einsum("ckij,qj->ckiq", d_field, t_tab, precision=high, preferred_element_type=jnp.float32)
    d_m = jnp.einsum("ip,ckiq->ckpq", r_tab[:height], d_left, precision=high, preferred_element_type=jnp.float32)

    dr, di = d_m[0], d_m[1]
    part = lambda x: (x[..., :HALF, :HALF], x[..., :HALF, HALF:], x[..., HALF:, :HALF], x[..., HALF:, HALF:])
    ra, rb, rc, rd = part(dr)
    ia, ib, ic, id_ = part(di)

    def spread(ee, eo, oe, oo):
        return join(ee + eo + oe + oo, ee - eo + oe - oo, ee + eo - oe - oo, ee - eo - oe + oo)

    dg_re = spread(ra, ib, ic, -rd)
    dg_im = spread(ia, -rb, -rc, -id_)
    ds_re = jnp.sum(h_re * dg_re + h_im * dg_im, 0)
    ds_im = jnp.sum(h_re * dg_im - h_im * dg_re, 0)
    ds_re, ds_im = lax.psum((ds_re, ds_im), ("kern", "row"))
    block = jnp.concatenate([jnp.concatenate([ds_re, -ds_im], 1), jnp.concatenate([-ds_im, -ds_re], 1)], 0) * scale
    grad = mm_tb(mm(row_tab, block), col_tab)
    gradient = grad * (1.0 - transmit * transmit)
    return gradient, resist[:height, :breadth]


def solution(mesh):
    return jax.shard_map(
        body,
        mesh=mesh,
        in_specs=(
            P(("grp", "row"), "kern"),
            P(("grp", "row"), "kern"),
            P(("grp", "row"), "kern"),
            P(),
            P("kern"),
            P(None, "kern", None, None),
        ),
        out_specs=(P(("grp", "row"), "kern"), P(("grp", "row"), "kern")),
        check_vma=False,
    )
```

time: 552 us -> 372 us (0.67)
  matrix products: 212 us -> 64.1 us
  other arithmetic: 74.8 us -> 38.5 us
  local copies, waits for them, and re-layouts: 30.6 us -> 62.9 us
  waiting for transfers between devices: 188 us -> 173 us
  starting transfers between devices: 21.5 us -> 11 us
    dot_general x23 -> x10, matrix products: 212 us -> 64.1 us  [the longest x1 20.7 us: body(): jnp.einsum('ckiq,qj->ckij', left_part, t_tab, precision=high, preferred_e...]
    rev x0 -> x2, local copies, waits for them, and re-layouts: none -> 21.9 us  [the longest x1 11.6 us: fold(): return jnp.concatenate([h[..., HALF:], jnp.flip(h[..., :HALF], -1)], -1)]
    add x10 -> x9, other arithmetic: 32.7 us -> 14.4 us  [the longest x6 13.5 us: diffuse(): return acid + root * up]
    mul x3 -> x4, other arithmetic: 21.5 us -> 5.98 us  [the longest x1 3.48 us: body(): sens = 2.0 * steepness * resist * (1.0 - resist) * (resist - target)]
    slice x4 -> x44, local copies, waits for them, and re-layouts: 4.3 us -> 18.5 us  [the longest x2 4.25 us: body(): u_tab = jnp.concatenate([u_mid[LANES // 2:], u_mid[:LANES // 2]], 0)]
    sin x1 -> x0, other arithmetic: 10.4 us -> none  [dft_tables(): return (jnp.cos(angles), jnp.sin(angles))]
    all_gather x1 -> x0, waiting for transfers between devices: 10.2 us -> none  [body(): lax.all_gather(sensitivity, 'kern', axis=1, tiled=True)]
    ppermute x8 -> x4, starting transfers between devices: 21 us -> 10.8 us  [the longest x1 5.16 us: body(): above = lax.ppermute(both[:, height - HALO:], 'row', up)]
  transfers between devices with their start and end apart: 12 -> 8, of which waited for: 9 -> 6; matrix products, arithmetic and copies ran while one was open for 5% -> 15% of each run, Pallas kernels for 0% -> 0%
where the time goes in v1:
time: 372 us; the launch traced here: 365 us
  waiting for transfers between devices  173 us (47%)
  matrix products  64.1 us (17%)
  local copies, waits for them, and re-layouts  62.9 us (17%)
  other arithmetic  38.5 us (10%)
  between operations  14.9 us (4%)
  starting transfers between devices  11 us (3%)
    psum x1, waiting for transfers between devices, body(): ds_re, ds_im = lax.psum((ds_re, ds_im), ('kern', 'row'))  90.3 us
    psum x1, waiting for transfers between devices, body(): s_re, s_im = lax.psum((s_re, s_im), ('kern', 'row'))  42.1 us
    dot_general x1, matrix products, body(): jnp.einsum('ckiq,qj->ckij', left_part, t_tab, precision=high, preferred_e...  20.7 us
    psum x1, waiting for transfers between devices, body(): q_grid = lax.psum(q_grid, 'kern')  20 us
    psum x1, waiting for transfers between devices, body(): power = lax.psum(power, 'kern')  17.8 us
    add x6, other arithmetic, diffuse(): return acid + root * up  13.5 us
    unnamed x46, local copies, waits for them, and re-layouts  12.4 us
    dot_general x3, matrix products, mm(): return jnp.dot(a, b, precision=high, preferred_element_type=jnp.float32)  12.3 us
  transfers between devices with their start and end apart: 8, of which 6 were waited for; matrix products, arithmetic and copies ran while one was open for 15% of the time, Pallas kernels for 0%

profile of v1, /device:TPU:0, one launch (start us, length us, event | category | flops | bytes accessed | tf_op | source)
XLA Modules:
  0.0 364.6 jit_solution(8749746412425415881)
XLA Ops:
  7.2 0.7 sqrt.3
  7.9 0.8 select_reduce_fusion
  8.6 2.6 broadcast_in_dim.2
  11.2 3.8 %stack_reshape.3 = f32[1,256,1024]{2,1,0:T(8,128)S(1)} reshape(f32[8,32,32,32]{3,2,1,0:T(8,128)} %broadcast_in_dim.2) | data formatting | bytes 2097152 | tf_op jit(solution)/shard_map/stack;reshape | solution.py:113
  15.1 0.9 fusion.142
  16.0 3.1 collective-permute-start.1
  19.0 1.3 collective-permute-start
  20.3 5.0 %fusion.14 = f32[512,256]{1,0:T(8,128)S(1)} fusion(f32[2048,512]{1,0:T(8,128)} %constant.47.clone, s32[]{:T(128)S(6)} %select_n.13, f32[256,1024]{1,0:T(8,128)S(1)} %copy-done.14), kind=kOutput, calls=%fused_computation.21 | convolution fusion | flops 1610612736 | bytes 3670020 | tf_op jit(solution)/shard_map/dot_general | solution.py:21
  25.4 2.9 fusion.136
  28.3 0.9 fusion.145
  29.2 1.5 pad_maximum_fusion
  30.7 0.9 constant_dynamic-slice_fusion
  31.6 3.3 constant_dynamic-slice_fusion.1
  35.0 1.7 fusion.160
  36.7 10.3 %rev.8 = f32[2,8,128,256]{3,2,1,0:T(8,128)} reverse(f32[2,8,128,256]{3,2,1,0:T(8,128)S(1)} %get-tuple-element.26), dimensions={2} | reverse | bytes 4194304 | tf_op jit(solution)/shard_map/jit(_flip)/rev | solution.py:58
  47.0 4.0 %fusion.22 = (f32[2,8,256,128]{3,2,1,0:T(8,128)}, f32[2,8,256,128]{3,2,1,0:T(8,128)S(1)}) fusion(f32[2,8,128,256]{3,2,1,0:T(8,128)} %get-tuple-element.25, f32[2,8,128,256]{3,2,1,0:T(8,128)} %rev.8), kind=kLoop, calls=%fused_computation.36 | loop fusion | flops 1048576 | bytes 8388608 | tf_op jit(solution)/shard_map/concatenate | solution.py:58
  51.0 0.7 constant_dynamic-slice_fusion.2
  51.7 11.6 %rev.9 = f32[2,8,256,128]{3,2,1,0:T(8,128)} reverse(f32[2,8,256,128]{3,2,1,0:T(8,128)S(1)} %get-tuple-element.24), dimensions={3} | reverse | bytes 4194304 | tf_op jit(solution)/shard_map/jit(_flip)/rev | solution.py:59
  63.3 1.7 constant_dynamic-slice_fusion.3
  65.0 2.6 concatenate.213
  67.6 1.3 collective-permute-start.2
  68.9 5.2 %collective-permute-start.3 = (f32[2,8,1152]{2,1,0:T(8,128)S(1)}, f32[2,8,1152]{2,1,0:T(8,128)S(1)}, u32[]{:S(2)}, u32[]{:S(2)}) collective-permute-start(f32[2,8,1152]{2,1,0:T(8,128)S(1)} %get-tuple-element.30), channel_id=1, source_target_pairs={{0,1},{1,2},{2,3},{3,4},{4,5},{5,6},{6,7},{8,9},{9,10},{10,11},{11... | collective-permute-start | bytes 221192 | tf_op jit(solution)/shard_map/ppermute | solution.py:122
  74.3 2.8 collective-permute-done.3
  77.0 1.8 pad_maximum_fusion.1
  79.0 1.9 fusion.195
  80.9 42.1 %all-reduce.13.cloned.1.call-done = (f32[256,256]{1,0:T(8,128)}, f32[256,256]{1,0:T(8,128)}) async-done(((f32[256,256]{1,0:T(8,128)}, f32[256,256]{1,0:T(8,128)}), (f32[256,256]{1,0:T(8,128)}, f32[256,256]{1,0:T(8,128)})) %all-reduce.13.cloned.1.call-update) | async-done | bytes 524304 | tf_op jit(solution)/shard_map/psum | solution.py:107
  123.0 2.9 multiply_subtract_fusion
  126.3 1.0 copy-done.7
  127.3 0.7 copy-done.9
  128.9 0.6 copy-done.18
  129.5 4.2 %fusion.7 = f32[2,8,256,272]{2,3,1,0:T(8,128)S(1)} fusion(f32[1,8,256,256]{3,2,1,0:T(8,128)S(1)} %get-tuple-element.114, f32[1,8,256,256]{3,2,1,0:T(8,128)S(1)} %get-tuple-element.113, f32[8,256]{1,0:T(8,128)S(1)} %constant_dynamic-slice_fusion.2, f32[264,256]{1,0:T(8,128)S(1)} %copy-done.18), kind=kOutput, calls=%fused_computation.14 | convolution fusion | flops 3423670272 | bytes 8929280 | tf_op jit(solution)/shard_map/ip,ckpq->ckiq/dot_general | solution.py:133
  133.8 20.7 %fusion.5 = f32[2,8,272,512]{3,2,1,0:T(8,128)S(1)} fusion(f32[256,512,1,1]{1,0,3,2:T(8,128)S(1)} %copy-done.17, f32[2,8,256,272]{2,3,1,0:T(8,128)S(1)} %fusion.7), kind=kOutput, calls=%fused_computation.8 | convolution fusion | flops 6845104128 | bytes 13893632 | tf_op jit(solution)/shard_map/ckiq,qj->ckij/dot_general | solution.py:134
  154.5 3.5 copy-done.4
  158.0 2.0 fusion.4
  160.1 1.6 slice_bitcast_fusion.4
  161.7 17.8 %all-reduce.7.cloned.1.call-done = f32[272,512]{1,0:T(8,128)} async-done(((f32[272,512]{1,0:T(8,128)}), f32[272,512]{1,0:T(8,128)}) %all-reduce.7.cloned.1.call-update) | async-done | bytes 557072 | tf_op jit(solution)/shard_map/psum | solution.py:136
  179.5 4.3 %fusion.16 = f32[272,1152]{1,0:T(8,128)S(1)} fusion(f32[272,512]{1,0:T(8,128)} %all-reduce.7.cloned.1.call-done, f32[64,512]{1,0:T(8,128)S(1)} %constant_dynamic-slice_fusion, f32[1088,512]{1,0:T(8,128)} %constant_dynamic-slice_fusion.1), kind=kOutput, calls=%fused_computation.29 | convolution fusion | flops 1925775360 | bytes 4169728 | tf_op jit(solution)/shard_map/dot_general | solution.py:29
  184.6 0.9 copy-done
  186.5 2.2 fusion.36
  189.4 2.2 fusion.45
  192.4 2.2 fusion.54
  194.7 0.4 fusion.181
  195.3 3.5 fusion.30
  199.5 2.3 fusion.78
  202.5 2.2 fusion.87
  205.4 2.4 fusion.96
  207.9 0.4 fusion.164
  208.8 1.0 copy-done.6
  209.8 5.0 %fusion.23 = f32[256,512]{1,0:T(8,128)} fusion(f32[2176,512]{1,0:T(8,128)} %constant.50.clone, s32[]{:T(128)S(6)} %add.266, f32[272,1151]{1,0:T(8,128)S(1)} %copy-done.1, f32[272,1151]{1,0:T(8,128)S(1)} %copy-done, f32[271,1152]{1,0:T(8,128)S(1)} %copy-done.3, f32[271,1152]{1,0:T(8,128)S(1)} %copy-done.2, f32[272,1]{1,0:T(8,128)S(1)} %get-tuple-element.50, ...), kind=kOutput, calls=%fused_computation.39 | convolution fusion | flops 1615069184 | bytes 14902276 | tf_op jit(solution)/shard_map/dot_general | solution.py:21
  214.9 20.0 %all-reduce.9.cloned.1.call-done = f32[256,512]{1,0:T(8,128)} async-done(((f32[256,512]{1,0:T(8,128)}), f32[256,512]{1,0:T(8,128)}) %all-reduce.9.cloned.1.call-update) | async-done | bytes 524304 | tf_op jit(solution)/shard_map/psum | solution.py:145
  234.9 1.6 broadcast_multiply_fusion
  236.5 10.3 %fusion = f32[2,8,256,256]{2,3,1,0:T(8,128)S(1)} fusion(f32[256,512,1,1]{1,0,3,2:T(8,128)S(1)} %copy-done.17, f32[2,8,272,512]{3,2,1,0:T(8,128)} %copy-done.4, f32[8,256,512]{2,1,0:T(8,128)S(1)} %broadcast_multiply_fusion), kind=kOutput, calls=%fused_computation.1 | convolution fusion | flops 6444548096 | bytes 17301504 | tf_op jit(solution)/shard_map/ckij,qj->ckiq/dot_general | solution.py:147
  246.8 4.9 %convolution_bitcast_fusion = f32[2,8,256,256]{3,2,1,0:T(8,128)S(1)} fusion(f32[2,8,256,256]{2,3,1,0:T(8,128)S(1)} %fusion, f32[2064,256]{1,0:T(8,128)} %constant.48.clone, s32[]{:T(128)S(6)} %add.265), kind=kOutput, calls=%fused_computation.33 | convolution fusion | flops 3221225472 | bytes 8650756 | tf_op jit(solution)/shard_map/ip,ckiq->ckpq/dot_general | solution.py:148
  252.8 1.2 copy-done.8
  254.0 0.6 copy-done.10
  254.7 1.1 subtract_reduce_fusion
  255.8 0.8 copy.31
  256.6 0.8 copy.30
  257.5 1.1 slice.679
  258.6 90.3 %all-reduce.11.cloned.1.call-done = (f32[256,256]{0,1:T(8,128)}, f32[256,256]{0,1:T(8,128)}) async-done(((f32[256,256]{0,1:T(8,128)}, f32[256,256]{0,1:T(8,128)}), (f32[256,256]{0,1:T(8,128)}, f32[256,256]{0,1:T(8,128)})) %all-reduce.11.cloned.1.call-update) | async-done | bytes 524304 | tf_op jit(solution)/shard_map/psum | solution.py:162
  348.9 1.0 neg.47
  349.9 1.0 neg.48
  350.8 2.3 fusion.127
  353.1 4.5 %fusion.26 = f32[256,1024]{1,0:T(8,128)} fusion(f32[256,512]{1,0:T(8,128)S(1)} %fusion.127, f32[2048,512]{1,0:T(8,128)} %constant.47.clone, s32[]{:T(128)S(6)} %select_n.13, f32[256,1024]{1,0:T(8,128)S(1)} %copy-done.15), kind=kOutput, calls=%fused_computation.61 | convolution fusion | flops 1611399168 | bytes 4718596 | tf_op jit(solution)/shard_map/dot_general | solution.py:29
  (91 shorter events, 9.0 us)
Async XLA Ops:
  7.2 115.8 %all-reduce.13.cloned.1.call-start = ((), (), s32[]{:S(2)}) async-start(), calls=%async_computation.3 | async-start | bytes 1048576 | tf_op jit(solution)/shard_map/psum | solution.py:107
  11.2 3.9 %copy-start.16 = (f32[256,1024]{1,0:T(8,128)S(1)}, f32[256,1024]{1,0:T(8,128)}, u32[]{:S(2)}) copy-start(f32[256,1024]{1,0:T(8,128)} %param.12) | copy-start | bytes 3145732
  15.1 5.2 %copy-start.14 = (f32[256,1024]{1,0:T(8,128)S(1)}, f32[256,1024]{1,0:T(8,128)}, u32[]{:S(2)}) copy-start(f32[256,1024]{1,0:T(8,128)} %param.11) | copy-start | bytes 3145732
  16.0 49.0 %collective-permute-start.1 = (f32[2,256,64]{2,1,0:T(8,128)}, f32[2,256,64]{2,1,0:T(8,128)}, u32[]{:S(2)}, u32[]{:S(2)}) collective-permute-start(f32[2,256,64]{2,1,0:T(8,128)} %get-tuple-element.31), channel_id=1, source_target_pairs={{0,8},{1,9},{2,10},{3,11},{4,12},{5,13},{6,14},{7,15},{16,24},{17,... | collective-permute-start | bytes 393224 | tf_op jit(solution)/shard_map/ppermute | solution.py:117
  19.0 46.0 %collective-permute-start = (f32[2,256,64]{2,1,0:T(8,128)}, f32[2,256,64]{2,1,0:T(8,128)}, u32[]{:S(2)}, u32[]{:S(2)}) collective-permute-start(f32[2,256,64]{2,1,0:T(8,128)} %get-tuple-element.32), channel_id=1, source_target_pairs={{8,0},{9,1},{10,2},{11,3},{12,4},{13,5},{14,6},{15,7},{24,16},{25,... | collective-permute-start | bytes 393224 | tf_op jit(solution)/shard_map/ppermute | solution.py:116
  29.2 150.3 %all-reduce.7.cloned.1.call-start = ((), (), s32[]{:S(2)}) async-start(), calls=%async_computation | async-start | bytes 1114112 | tf_op jit(solution)/shard_map/psum | solution.py:136
  31.6 3.4 copy-start.13
  67.6 6.6 %copy-start.11 = (f32[2,256,1152]{2,1,0:T(8,128)}, f32[2,256,1152]{2,1,0:T(8,128)S(1)}, u32[]{:S(2)}) copy-start(f32[2,256,1152]{2,1,0:T(8,128)S(1)} %concatenate.213) | copy-start | bytes 7077892
  67.6 6.6 %collective-permute-start.2 = (f32[2,8,1152]{2,1,0:T(8,128)S(1)}, f32[2,8,1152]{2,1,0:T(8,128)S(1)}, u32[]{:S(2)}, u32[]{:S(2)}) collective-permute-start(f32[2,8,1152]{2,1,0:T(8,128)S(1)} %get-tuple-element.29), channel_id=1, source_target_pairs={{1,0},{2,1},{3,2},{4,3},{5,4},{6,5},{7,6},{9,8},{10,9},{11,10},{12... | collective-permute-start | bytes 221192 | tf_op jit(solution)/shard_map/ppermute | solution.py:121
  68.9 8.1 %collective-permute-start.3 = (f32[2,8,1152]{2,1,0:T(8,128)S(1)}, f32[2,8,1152]{2,1,0:T(8,128)S(1)}, u32[]{:S(2)}, u32[]{:S(2)}) collective-permute-start(f32[2,8,1152]{2,1,0:T(8,128)S(1)} %get-tuple-element.30), channel_id=1, source_target_pairs={{0,1},{1,2},{2,3},{3,4},{4,5},{5,6},{6,7},{8,9},{9,10},{10,11},{11... | collective-permute-start | bytes 221192 | tf_op jit(solution)/shard_map/ppermute | solution.py:122
  78.9 1.9 copy-start.5
  125.9 1.3 copy-start.7
  125.9 2.0 copy-start.9
  126.0 2.0 copy-start.19
  126.0 2.0 copy-start.20
  128.6 1.0 copy-start.18
  129.5 4.2 %copy-start.17 = (f32[256,512,1,1]{1,0,3,2:T(8,128)S(1)}, f32[256,512,1,1]{1,0,3,2:T(8,128)}, u32[]{:S(2)}) copy-start(f32[256,512,1,1]{1,0,3,2:T(8,128)} %constant.52) | copy-start | bytes 1572868
  133.8 24.2 %copy-start.21 = (f32[8]{0:T(128)S(1)}, f32[8]{0:T(128)}, u32[]{:S(2)}) copy-start(f32[8]{0:T(128)} %param.15) | copy-start | bytes 100
  154.5 3.5 copy-start.4
  160.0 74.9 %all-reduce.9.cloned.1.call-start = ((), (), s32[]{:S(2)}) async-start(), calls=%async_computation.1 | async-start | bytes 1048576 | tf_op jit(solution)/shard_map/psum | solution.py:145
  184.1 1.3 copy-start
  184.1 1.7 copy-start.1
  184.1 2.0 copy-start.2
  184.1 2.4 copy-start.3
  208.5 1.3 copy-start.6
  214.8 134.1 %all-reduce.11.cloned.1.call-start = ((), (), s32[]{:S(2)}) async-start(), calls=%async_computation.2 | async-start | bytes 1048576 | tf_op jit(solution)/shard_map/psum | solution.py:162
  252.4 1.6 copy-start.8
  252.4 2.2 copy-start.10
  255.8 1.7 copy-start.12
  350.8 2.3 copy-start.15
Sparse Core Ops, SparseCore 0:
  29.3 93.6 all-reduce.12
  160.1 19.3 all-reduce.6
  214.9 19.9 all-reduce.8
  257.6 91.2 all-reduce.10

commit v2 on v1

v2 whole, which is shorter than its diff:
```python
import numpy as np
import jax
import jax.numpy as jnp
from jax import lax
from jax.experimental import pallas as pl
from jax.experimental.pallas import tpu as pltpu
from jax.sharding import PartitionSpec as P

PIXELS = 2048
BAND = 256
BLOCK = 32
STEPS = 4
HALF = BAND // 2
GRID = 2 * BAND
HALO = 2 * STEPS
LANES = 128
steepness = 8.0
threshold = 0.5
MESH = pl.DeviceIdType.MESH
NN = ((1,), (0,))
NT = ((1,), (1,))
TN = ((0,), (0,))


def mask_table():
    n = np.arange(HALF)
    f = np.concatenate([n, -(n + 1)])
    angle = 2 * np.pi / PIXELS * ((f[:, None] * np.arange(PIXELS)[None, :]) % PIXELS)
    return np.cos(angle), np.sin(angle)


def half_table(positions):
    n = np.arange(HALF)
    angle = np.pi / PIXELS * (((2 * n + 1)[:, None] * positions[None, :]) % (2 * PIXELS))
    return np.concatenate([np.cos(angle), np.sin(angle)], 0)


def interpolation_table():
    d = np.arange(PIXELS)[:, None] - (PIXELS // GRID) * np.arange(GRID)[None, :]
    d = d % PIXELS
    safe = np.where(d == 0, 1, d)
    u = np.sin(2 * np.pi * ((BAND * safe) % PIXELS) / PIXELS) / (GRID * np.tan(np.pi * safe / PIXELS))
    return np.where(d == 0, 1.0, u)


def halves(x):
    x = x.astype(np.float32)
    hi = x.astype(jnp.bfloat16)
    lo = (x - hi.astype(np.float32)).astype(jnp.bfloat16)
    return jnp.asarray(hi), jnp.asarray(lo)


def fold_matrix():
    a = np.arange(BAND)
    p = np.zeros((BAND, BAND))
    p[a, np.where(a < HALF, a + HALF, BAND - 1 - a)] = 1.0
    return jnp.asarray(p.astype(jnp.bfloat16)), jnp.asarray(p.T.astype(jnp.bfloat16))


def quads(g):
    a, b, c, d = g[..., :HALF, :HALF], g[..., :HALF, HALF:], g[..., HALF:, :HALF], g[..., HALF:, HALF:]
    return a + b + c + d, a + c - b - d, a + b - c - d, a - b - c + d


def join(a, b, c, d):
    return jnp.concatenate([jnp.concatenate([a, b], -1), jnp.concatenate([c, d], -1)], -2)


def spread(ee, eo, oe, oo):
    return join(ee + eo + oe + oo, ee - eo + oe - oo, ee + eo - oe - oo, ee - eo - oe + oo)


def split(x):
    hi = x.astype(jnp.bfloat16)
    return hi, (x - hi.astype(jnp.float32)).astype(jnp.bfloat16)


def dot(a, b, dims):
    return lax.dot_general(a, b, (dims, ((), ())), preferred_element_type=jnp.float32)


def dot3(a, b, dims=NN):
    return dot(a[0], b[0], dims) + dot(a[0], b[1], dims) + dot(a[1], b[0], dims)


def diffuse(acid, vertical, across):
    fv = vertical * (pltpu.roll(acid, 1, 0) - acid)
    fh = across * (pltpu.roll(acid, 1, 1) - acid)
    tall, wide = acid.shape
    return acid + (fv - pltpu.roll(fv, tall - 1, 0)) + (fh - pltpu.roll(fh, wide - 1, 1))


def kernel(rows_n, mask, target, root_rows, weights, spectra, m_hi, m_lo, u_hi, u_lo, t_hi, t_lo, r_all, p_fwd, p_bwd,
           gradient, resist_out,
           spec, full1, full2, pair_in, part, rs_in, both, h_in, h, fields, power, power_in, grid, grid_in,
           row_hi, row_lo, col_hi, col_lo, ut_hi, ut_lo, r_buf, transmit,
           local_sem, pair_send, pair_recv, rs_send, rs_recv, ag_send, ag_recv):
    height, breadth = mask.shape
    tall, wide = both.shape[1:]
    kernels = h.shape[1]
    row, col = lax.axis_index("row"), lax.axis_index("kern")
    partner = 1 - col
    row_start, col_start = row * height, pl.multiple_of(col * breadth, LANES)
    slab = pl.multiple_of(breadth - LANES * col, LANES)

    local = [
        pltpu.make_async_copy(m_hi.at[pl.ds(col_start, breadth)], col_hi, local_sem.at[0]),
        pltpu.make_async_copy(m_lo.at[pl.ds(col_start, breadth)], col_lo, local_sem.at[1]),
        pltpu.make_async_copy(m_hi.at[pl.ds(row_start, height)], row_hi, local_sem.at[2]),
        pltpu.make_async_copy(m_lo.at[pl.ds(row_start, height)], row_lo, local_sem.at[3]),
        pltpu.make_async_copy(spectra, h_in, local_sem.at[4]),
        pltpu.make_async_copy(r_all.at[pl.ds(row_start + HALO, tall - HALO)], r_buf.at[pl.ds(0, tall - HALO)], local_sem.at[5]),
        pltpu.make_async_copy(r_all.at[pl.ds(row_start, HALO)], r_buf.at[pl.ds(tall - HALO, HALO)], local_sem.at[6]),
        pltpu.make_async_copy(u_hi.at[:, pl.ds(col_start, breadth)], ut_hi.at[:, pl.ds(0, breadth)], local_sem.at[7]),
        pltpu.make_async_copy(u_lo.at[:, pl.ds(col_start, breadth)], ut_lo.at[:, pl.ds(0, breadth)], local_sem.at[8]),
        pltpu.make_async_copy(u_hi.at[:, pl.ds(slab, LANES)], ut_hi.at[:, pl.ds(breadth, LANES)], local_sem.at[9]),
        pltpu.make_async_copy(u_lo.at[:, pl.ds(slab, LANES)], ut_lo.at[:, pl.ds(breadth, LANES)], local_sem.at[10]),
    ]
    for copy in local:
        copy.start()

    barrier = pltpu.get_barrier_semaphore()
    pl.semaphore_signal(barrier, inc=1, device_id={"kern": partner}, device_id_type=MESH)
    for o in range(1, rows_n):
        pl.semaphore_signal(barrier, inc=1, device_id={"row": lax.rem(row + o, rows_n)}, device_id_type=MESH)

    both[0, pl.ds(0, height), pl.ds(0, breadth)] = target[...]
    for b in range(root_rows.shape[0]):
        both[1, pl.ds(b * BLOCK, BLOCK), pl.ds(0, breadth)] = jnp.broadcast_to(root_rows[b : b + 1, :], (BLOCK, breadth))
    pl.semaphore_wait(barrier, rows_n)

    def to_pair(src, dst, n):
        return pltpu.make_async_remote_copy(
            src_ref=src, dst_ref=dst, send_sem=pair_send.at[n], recv_sem=pair_recv.at[n],
            device_id={"kern": partner}, device_id_type=MESH)

    edge = pl.multiple_of((breadth - LANES) * partner, LANES)
    side = to_pair(both.at[:, pl.ds(0, height), pl.ds(edge, LANES)], both.at[:, pl.ds(0, height), pl.ds(breadth, LANES)], 0)
    side.start()

    def to_row(src, dst, peer, send, recv, n):
        return pltpu.make_async_remote_copy(
            src_ref=src, dst_ref=dst, send_sem=send.at[n], recv_sem=recv.at[n],
            device_id={"row": peer}, device_id_type=MESH)

    chunk = BAND // rows_n

    def allreduce(at, src, full, beside_pair=None, beside_scatter=None, beside_gather=None):
        swap = to_pair(src.at[pl.ds(partner * BAND, BAND)], pair_in.at[at], 1 + 2 * at)
        swap.start()
        if beside_pair is not None:
            beside_pair()
        swap.wait()
        part[at] = src[pl.ds(col * BAND, BAND)] + pair_in[at]
        copies = []
        for o in range(1, rows_n):
            peer = lax.rem(row + o, rows_n)
            copies.append(to_row(part.at[at, pl.ds(peer * chunk, chunk)], rs_in.at[at, o - 1], peer, rs_send.at[at], rs_recv.at[at], o - 1))
            copies[-1].start()
        if beside_scatter is not None:
            beside_scatter()
        for copy in copies:
            copy.wait()
        total = part[at, pl.ds(row * chunk, chunk)]
        for o in range(1, rows_n):
            total = total + rs_in[at, o - 1]
        mine = pl.ds(col * BAND + row * chunk, chunk)
        full[mine] = total
        copies = []
        for o in range(1, rows_n):
            peer = lax.rem(row + o, rows_n)
            copies.append(to_row(full.at[mine], full.at[mine], peer, ag_send.at[at], ag_recv.at[at], o - 1))
            copies[-1].start()
        if beside_gather is not None:
            beside_gather()
        for copy in copies:
            copy.wait()
        half = pl.ds(col * BAND, BAND)
        swap = to_pair(full.at[half], full.at[half], 2 + 2 * at)
        swap.start()
        swap.wait()

    scale = 1.0 / (PIXELS * BAND)
    transmit[...] = jnp.tanh(mask[...])
    for copy in local[:4]:
        copy.wait()
    col_tab = (col_hi[...], col_lo[...])
    row_tab = (row_hi[...], row_lo[...])
    halfway = dot3(split(transmit[...]), col_tab)
    prod = dot3(row_tab, split(halfway), TN)
    spec[pl.ds(0, BAND)] = (prod[:BAND, :BAND] - prod[BAND:, BAND:]) * scale
    spec[pl.ds(BAND, BAND)] = -(prod[BAND:, :BAND] + prod[:BAND, BAND:]) * scale

    def fold(first, count):
        def step(k, _):
            for c in range(2):
                hi, lo = split(h_in[c, k])
                mid = split(dot(p_fwd[...], hi, NN) + dot(p_fwd[...], lo, NN))
                h[c, k] = dot(mid[0], p_bwd[...], NN) + dot(mid[1], p_bwd[...], NN)
            return 0
        lax.fori_loop(first, first + count, step, 0)

    ends = []

    def beside_pair():
        side.wait()
        ends.append(to_row(both.at[:, pl.ds(0, HALO)], both.at[:, pl.ds(height, HALO)], lax.rem(row + rows_n - 1, rows_n), rs_send.at[2], rs_recv.at[2], 0))
        ends.append(to_row(both.at[:, pl.ds(height - HALO, HALO)], both.at[:, pl.ds(height + HALO, HALO)], lax.rem(row + 1, rows_n), rs_send.at[2], rs_recv.at[2], 1))
        for copy in ends:
            copy.start()
        for copy in local[4:]:
            copy.wait()

    allreduce(0, spec, full1, beside_pair, lambda: fold(0, kernels // 2), lambda: fold(kernels // 2, kernels - kernels // 2))

    t_tab = (t_hi[...], t_lo[...])
    r_tab = split(r_buf[...])
    power[...] = jnp.zeros_like(power)

    def forward(k, _):
        h_re, h_im = h[0, k], h[1, k]
        s_re, s_im = full1[pl.ds(0, BAND)], full1[pl.ds(BAND, BAND)]
        ee_r, eo_r, oe_r, oo_r = quads(h_re * s_re - h_im * s_im)
        ee_i, eo_i, oe_i, oo_i = quads(h_re * s_im + h_im * s_re)
        square = 0.0
        for c, m in enumerate((join(ee_r, -eo_i, -oe_i, -oo_r), join(ee_i, eo_r, oe_r, -oo_i))):
            field = dot3(split(dot3(r_tab, split(m))), t_tab)
            fields[k, c] = field
            square = square + field * field
        power[...] += weights[k] * square
        return 0

    lax.fori_loop(0, kernels, forward, 0)
    swap = to_pair(power, power_in, 5)
    swap.start()

    for copy in ends:
        copy.wait()
    at_row = lax.broadcasted_iota(jnp.int32, (tall, wide), 0)
    at_col = lax.broadcasted_iota(jnp.int32, (tall, wide), 1)
    first, last = row == 0, row == rows_n - 1
    outside = (at_row >= height + HALO) & first
    outside = outside | ((at_row >= height) & (at_row < height + HALO) & last)
    outside = outside | ((at_col >= breadth + LANES // 2) & (col == 0))
    outside = outside | ((at_col >= breadth) & (at_col < breadth + LANES // 2) & (col == 1))
    root = jnp.where(outside, 0.0, both[1])
    vertical = root * pltpu.roll(root, 1, 0)
    across = root * pltpu.roll(root, 1, 1)
    swap.wait()

    u_tab = (ut_hi[...], ut_lo[...])
    acid = dot3(split(power[...] + power_in[...]), u_tab)
    for _ in range(STEPS):
        acid = diffuse(acid, vertical, across)
    resist = 1.0 / (1.0 + jnp.exp(-steepness * (acid - threshold)))
    resist_out[...] = resist[:height, :breadth]
    sens = 2.0 * steepness * resist * (1.0 - resist) * (resist - both[0])
    for _ in range(STEPS):
        sens = diffuse(sens, vertical, across)
    grid[...] = dot3(split(sens[:height, :breadth]), (u_tab[0][:, :breadth], u_tab[1][:, :breadth]), NT)
    swap = to_pair(grid, grid_in, 6)
    swap.start()
    r_back = split(r_buf[pl.ds(0, height)].T)
    spec[...] = jnp.zeros_like(spec)
    swap.wait()
    grid[...] = 2.0 * (grid[...] + grid_in[...])

    def backward(k, _):
        parts = []
        for c in range(2):
            d = (weights[k] * grid[...]) * fields[k, c, pl.ds(0, height)]
            d = dot3(r_back, split(dot3(split(d), t_tab, NT)))
            parts.append((d[:HALF, :HALF], d[:HALF, HALF:], d[HALF:, :HALF], d[HALF:, HALF:]))
        (ra, rb, rc, rd), (ia, ib, ic, id_) = parts
        dg_re = spread(ra, ib, ic, -rd)
        dg_im = spread(ia, -rb, -rc, -id_)
        h_re, h_im = h[0, k], h[1, k]
        spec[pl.ds(0, BAND)] += h_re * dg_re + h_im * dg_im
        spec[pl.ds(BAND, BAND)] += h_re * dg_im - h_im * dg_re
        return 0

    lax.fori_loop(0, kernels, backward, 0)
    allreduce(1, spec, full2)
    ds_re, ds_im = full2[pl.ds(0, BAND)] * scale, full2[pl.ds(BAND, BAND)] * scale
    block = join(ds_re, -ds_im, -ds_im, -ds_re)
    grad = dot3(split(dot3(row_tab, split(block))), col_tab, NT)
    gradient[...] = grad * (1.0 - transmit[...] * transmit[...])


def body(mask_levels, target_image, diffusion_index, diffusion_table, kernel_weights, kernel_spectra):
    height, breadth = mask_levels.shape
    rows_n, cols_n = lax.axis_size("row"), lax.axis_size("kern")
    assert cols_n == 2
    tall, wide = height + 2 * HALO, breadth + LANES
    kernels = kernel_weights.shape[0]
    ct, st = mask_table()
    m_hi, m_lo = halves(np.concatenate([ct.T, st.T], 1))
    u_hi, u_lo = halves(interpolation_table().T)
    t_hi, t_lo = halves(half_table(np.arange(GRID) * (PIXELS // GRID)))
    r_all = jnp.asarray(half_table(np.arange(-HALO, PIXELS + HALO)).T.astype(np.float32))
    p_fwd, p_bwd = fold_matrix()
    hot = (diffusion_index[:, :, None] == jnp.arange(diffusion_table.shape[0], dtype=jnp.int32)).astype(jnp.float32)
    block_root = jnp.sum(hot * jnp.sqrt(diffusion_table), -1)
    root_rows = jnp.repeat(block_root, BLOCK, axis=1)
    f32, bf16 = jnp.float32, jnp.bfloat16
    vmem, hbm, smem = (pl.BlockSpec(memory_space=s) for s in (pltpu.VMEM, pl.ANY, pltpu.SMEM))
    V = pltpu.VMEM
    D = pltpu.SemaphoreType.DMA
    peers = max(rows_n - 1, 2)
    return pl.pallas_call(
        lambda *refs: kernel(rows_n, *refs),
        out_shape=(jax.ShapeDtypeStruct((height, breadth), f32),) * 2,
        in_specs=[vmem, vmem, vmem, smem, hbm, hbm, hbm, hbm, hbm, vmem, vmem, hbm, vmem, vmem],
        out_specs=(vmem, vmem),
        scratch_shapes=[
            V((2 * BAND, BAND), f32), V((2 * BAND, BAND), f32), V((2 * BAND, BAND), f32),
            V((2, BAND, BAND), f32), V((2, BAND, BAND), f32), V((2, peers, BAND // rows_n, BAND), f32),
            V((2, tall, wide), f32), V(kernel_spectra.shape, f32), V(kernel_spectra.shape, f32),
            V((kernels, 2, tall, GRID), f32), V((tall, GRID), f32), V((tall, GRID), f32),
            V((height, GRID), f32), V((height, GRID), f32),
            V((height, 2 * BAND), bf16), V((height, 2 * BAND), bf16),
            V((breadth, 2 * BAND), bf16), V((breadth, 2 * BAND), bf16),
            V((GRID, wide), bf16), V((GRID, wide), bf16), V((tall, BAND), f32), V((height, breadth), f32),
            D((11,)), D((7,)), D((7,)), D((3, peers)), D((3, peers)), D((2, peers)), D((2, peers)),
        ],
        compiler_params=pltpu.CompilerParams(collective_id=0, has_side_effects=True, vmem_limit_bytes=60 * 2**20),
        name="resist_gradient",
    )(mask_levels, target_image, root_rows, kernel_weights, kernel_spectra, m_hi, m_lo, u_hi, u_lo, t_hi, t_lo, r_all, p_fwd, p_bwd)


def solution(mesh):
    return jax.shard_map(
        body,
        mesh=mesh,
        in_specs=(
            P(("grp", "row"), "kern"),
            P(("grp", "row"), "kern"),
            P(("grp", "row"), "kern"),
            P(),
            P("kern"),
            P(None, "kern", None, None),
        ),
        out_specs=(P(("grp", "row"), "kern"), P(("grp", "row"), "kern")),
        check_vma=False,
    )
```

time: 372 us -> 88.6 us (0.24); the launches traced: 365 us -> 88.4 us
  waiting for transfers between devices: 173 us -> 0 us
  Pallas kernels: 0 us -> 82.1 us
  matrix products: 64.1 us -> 0 us
  local copies, waits for them, and re-layouts: 62.9 us -> 4.85 us
  other arithmetic: 38.5 us -> 0.77 us
  between operations: 14.9 us -> 0.66 us
  starting transfers between devices: 11 us -> 0 us
    psum x4 -> x0, waiting for transfers between devices: 170 us -> none  [the longest x1 90.3 us: body(): ds_re, ds_im = lax.psum((ds_re, ds_im), ('kern', 'row'))]
    pallas_call x0 -> x1, Pallas kernels: none -> 82.1 us  [body(): pl.pallas_call(lambda *refs: kernel(rows_n, *refs), out_shape=(jax.ShapeD...]
    dot_general x10 -> x0, matrix products: 64.1 us -> none  [the longest x1 20.7 us: body(): jnp.einsum('ckiq,qj->ckij', left_part, t_tab, precision=high, preferred_e...]
    rev x2 -> x0, local copies, waits for them, and re-layouts: 21.9 us -> none  [the longest x1 11.6 us: fold(): return jnp.concatenate([h[..., HALF:], jnp.flip(h[..., :HALF], -1)], -1)]
    slice x44 -> x0, local copies, waits for them, and re-layouts: 18.5 us -> none  [the longest x2 4.25 us: body(): u_tab = jnp.concatenate([u_mid[LANES // 2:], u_mid[:LANES // 2]], 0)]
    add x9 -> x0, other arithmetic: 14.4 us -> none  [the longest x6 13.5 us: diffuse(): return acid + root * up]
    ppermute x4 -> x0, starting transfers between devices: 10.8 us -> none  [the longest x1 5.16 us: body(): above = lax.ppermute(both[:, height - HALO:], 'row', up)]
    unnamed x46 -> x4, local copies, waits for them, and re-layouts: 12.4 us -> 3.37 us
  transfers between devices with their start and end apart: 8 -> 0, of which waited for: 6 -> 0; matrix products, arithmetic and copies ran while one was open for 15% -> 0% of each run, Pallas kernels for 0% -> 0%
where the time goes in v2:
time: 88.6 us; the launch traced here: 88.4 us
  Pallas kernels  82.1 us (93%)
  local copies, waits for them, and re-layouts  4.85 us (5%)
    pallas_call x1, Pallas kernels, body(): pl.pallas_call(lambda *refs: kernel(rows_n, *refs), out_shape=(jax.ShapeD...  82.1 us
    unnamed x4, local copies, waits for them, and re-layouts  3.37 us

profile of v2, /device:TPU:0, one launch (start us, length us, event | category | flops | bytes accessed | tf_op | source)
XLA Modules:
  0.0 88.4 jit_solution(5119691880276748595)
XLA Ops:
  0.6 0.7 sqrt.3
  1.3 0.8 select_reduce_fusion
  2.1 0.1 broadcast_in_dim.2
  2.2 0.7 reshape.9.refs_2_
  2.9 82.1 %resist_gradient.1 = (f32[256,1024]{1,0:T(8,128)}, f32[256,1024]{1,0:T(8,128)}) custom-call(f32[256,1024]{1,0:T(8,128)} %refs_0_.1, f32[256,1024]{1,0:T(8,128)} %refs_1_.1, f32[8,1024]{1,0:T(8,128)} %reshape.9.refs_2_, f32[8]{0:T(128)} %refs_3_.1, f32[2,8,256,256]{3,2,1,0:T(8,128)} %refs_4_.1, bf16[2048,512]{1,0:T(8,128)(2,1)} %constant.21.clone.refs_5_, ...), custom_call_target="tpu_custom_call" | custom-call | tf_op jit(solution)/shard_map/resist_gradient/pallas_call | solution.py:310
  85.0 0.0 copy-start
  85.0 2.4 %copy.19 = f32[256,1024]{1,0:T(8,128)} copy(f32[256,1024]{1,0:T(8,128)} %get-tuple-element.4) | data formatting | bytes 2097152
  87.4 0.0 copy-done
  87.4 1.0 %copy.20 = f32[256,1024]{1,0:T(8,128)} copy(f32[256,1024]{1,0:T(8,128)S(1)} %copy-done) | data formatting | bytes 2097152
Async XLA Ops:
  85.0 2.4 %copy-start = (f32[256,1024]{1,0:T(8,128)S(1)}, f32[256,1024]{1,0:T(8,128)}, u32[]{:S(2)}) copy-start(f32[256,1024]{1,0:T(8,128)} %get-tuple-element.5) | copy-start | bytes 3145732

commit v3 on v2

--- a/solution.py
+++ b/solution.py
@@ -83,16 +83,33 @@
     return dot(a[0], b[0], dims) + dot(a[0], b[1], dims) + dot(a[1], b[0], dims)
 
 
-def diffuse(acid, vertical, across):
-    fv = vertical * (pltpu.roll(acid, 1, 0) - acid)
-    fh = across * (pltpu.roll(acid, 1, 1) - acid)
-    tall, wide = acid.shape
-    return acid + (fv - pltpu.roll(fv, tall - 1, 0)) + (fh - pltpu.roll(fh, wide - 1, 1))
-
-
-def kernel(rows_n, mask, target, root_rows, weights, spectra, m_hi, m_lo, u_hi, u_lo, t_hi, t_lo, r_all, p_fwd, p_bwd,
+def diffuse(ping, pong, coefs):
+    tall, wide = ping.shape[0] - 2 * HALO, ping.shape[1]
+
+    def step(src, dst):
+        for at in range(HALO, HALO + tall, 16):
+            x = src[at : at + 16, :]
+            here = [c[at : at + 16, :] for c in coefs]
+            moved = here[0] * (src[at - 1 : at + 15, :] - x) + here[1] * (src[at + 1 : at + 17, :] - x)
+            moved = moved + here[2] * (pltpu.roll(x, 1, 1) - x) + here[3] * (pltpu.roll(x, wide - 1, 1) - x)
+            dst[at : at + 16, :] = x + moved
+
+    def twice(_, carry):
+        step(ping, pong)
+        step(pong, ping)
+        return carry
+
+    lax.fori_loop(0, STEPS // 2, twice, 0)
+
+
+def linear(x, height):
+    pad = jnp.zeros((HALO, x.shape[1]), x.dtype)
+    return jnp.concatenate([pad, x[height + HALO :], x[: height + HALO], pad], 0)
+
+
+def kernel(rows_n, mask, target, levels, level_values, weights, spectra, m_hi, m_lo, u_hi, u_lo, t_hi, t_lo, r_all, p_fwd, p_bwd,
            gradient, resist_out,
-           spec, full1, full2, pair_in, part, rs_in, both, h_in, h, fields, power, power_in, grid, grid_in,
+           spec, full1, full2, pair_in, part, rs_in, ping, pong, c_up, c_down, c_left, c_right, both, h_in, h, fields, power, power_in, grid, grid_in,
            row_hi, row_lo, col_hi, col_lo, ut_hi, ut_lo, r_buf, transmit,
            local_sem, pair_send, pair_recv, rs_send, rs_recv, ag_send, ag_recv):
     height, breadth = mask.shape
@@ -125,7 +142,19 @@
         pl.semaphore_signal(barrier, inc=1, device_id={"row": lax.rem(row + o, rows_n)}, device_id_type=MESH)
 
     both[0, pl.ds(0, height), pl.ds(0, breadth)] = target[...]
-    for b in range(root_rows.shape[0]):
+    index = levels[...]
+    value = jnp.zeros(index.shape, jnp.float32)
+    for n in range(level_values.shape[0]):
+        value = jnp.where(index == n, level_values[n], value)
+    value = jnp.sqrt(value)
+    block_at = lax.broadcasted_iota(jnp.int32, (index.shape[1], breadth), 0)
+    pixel_at = lax.broadcasted_iota(jnp.int32, (index.shape[1], breadth), 1)
+    inside = (pixel_at >= block_at * BLOCK) & (pixel_at < (block_at + 1) * BLOCK)
+    inside = jnp.where(inside, 1.0, 0.0).astype(jnp.bfloat16)
+    hi, lo = split(value)
+    rest = (value - hi.astype(jnp.float32) - lo.astype(jnp.float32)).astype(jnp.bfloat16)
+    root_rows = dot(hi, inside, NN) + dot(lo, inside, NN) + dot(rest, inside, NN)
+    for b in range(index.shape[0]):
         both[1, pl.ds(b * BLOCK, BLOCK), pl.ds(0, breadth)] = jnp.broadcast_to(root_rows[b : b + 1, :], (BLOCK, breadth))
     pl.semaphore_wait(barrier, rows_n)
 
@@ -230,7 +259,7 @@
         power[...] += weights[k] * square
         return 0
 
-    lax.fori_loop(0, kernels, forward, 0)
+    lax.fori_loop(0, kernels, forward, 0, unroll=2)
     swap = to_pair(power, power_in, 5)
     swap.start()
 
@@ -244,20 +273,26 @@
     outside = outside | ((at_col >= breadth + LANES // 2) & (col == 0))
     outside = outside | ((at_col >= breadth) & (at_col < breadth + LANES // 2) & (col == 1))
     root = jnp.where(outside, 0.0, both[1])
-    vertical = root * pltpu.roll(root, 1, 0)
-    across = root * pltpu.roll(root, 1, 1)
+    root = linear(root, height)
+    rows_all = tall + 2 * HALO
+    c_up[...] = root * pltpu.roll(root, 1, 0)
+    c_down[...] = root * pltpu.roll(root, rows_all - 1, 0)
+    c_left[...] = root * pltpu.roll(root, 1, 1)
+    c_right[...] = root * pltpu.roll(root, wide - 1, 1)
+    coefs = (c_up, c_down, c_left, c_right)
+    pong[...] = jnp.zeros_like(pong)
     swap.wait()
 
     u_tab = (ut_hi[...], ut_lo[...])
     acid = dot3(split(power[...] + power_in[...]), u_tab)
-    for _ in range(STEPS):
-        acid = diffuse(acid, vertical, across)
-    resist = 1.0 / (1.0 + jnp.exp(-steepness * (acid - threshold)))
-    resist_out[...] = resist[:height, :breadth]
-    sens = 2.0 * steepness * resist * (1.0 - resist) * (resist - both[0])
-    for _ in range(STEPS):
-        sens = diffuse(sens, vertical, across)
-    grid[...] = dot3(split(sens[:height, :breadth]), (u_tab[0][:, :breadth], u_tab[1][:, :breadth]), NT)
+    ping[...] = linear(acid, height)
+    diffuse(ping, pong, coefs)
+    resist = 1.0 / (1.0 + jnp.exp(-steepness * (ping[...] - threshold)))
+    resist_out[...] = resist[2 * HALO : 2 * HALO + height, :breadth]
+    ping[...] = 2.0 * steepness * resist * (1.0 - resist) * (resist - linear(both[0], height))
+    diffuse(ping, pong, coefs)
+    sens = ping[pl.ds(2 * HALO, height), pl.ds(0, breadth)]
+    grid[...] = dot3(split(sens), (u_tab[0][:, :breadth], u_tab[1][:, :breadth]), NT)
     swap = to_pair(grid, grid_in, 6)
     swap.start()
     r_back = split(r_buf[pl.ds(0, height)].T)
@@ -279,7 +314,7 @@
         spec[pl.ds(BAND, BAND)] += h_re * dg_im - h_im * dg_re
         return 0
 
-    lax.fori_loop(0, kernels, backward, 0)
+    lax.fori_loop(0, kernels, backward, 0, unroll=2)
     allreduce(1, spec, full2)
     ds_re, ds_im = full2[pl.ds(0, BAND)] * scale, full2[pl.ds(BAND, BAND)] * scale
     block = join(ds_re, -ds_im, -ds_im, -ds_re)
@@ -299,9 +334,6 @@
     t_hi, t_lo = halves(half_table(np.arange(GRID) * (PIXELS // GRID)))
     r_all = jnp.asarray(half_table(np.arange(-HALO, PIXELS + HALO)).T.astype(np.float32))
     p_fwd, p_bwd = fold_matrix()
-    hot = (diffusion_index[:, :, None] == jnp.arange(diffusion_table.shape[0], dtype=jnp.int32)).astype(jnp.float32)
-    block_root = jnp.sum(hot * jnp.sqrt(diffusion_table), -1)
-    root_rows = jnp.repeat(block_root, BLOCK, axis=1)
     f32, bf16 = jnp.float32, jnp.bfloat16
     vmem, hbm, smem = (pl.BlockSpec(memory_space=s) for s in (pltpu.VMEM, pl.ANY, pltpu.SMEM))
     V = pltpu.VMEM
@@ -310,11 +342,12 @@
     return pl.pallas_call(
         lambda *refs: kernel(rows_n, *refs),
         out_shape=(jax.ShapeDtypeStruct((height, breadth), f32),) * 2,
-        in_specs=[vmem, vmem, vmem, smem, hbm, hbm, hbm, hbm, hbm, vmem, vmem, hbm, vmem, vmem],
+        in_specs=[vmem, vmem, vmem, smem, smem, hbm, hbm, hbm, hbm, hbm, vmem, vmem, hbm, vmem, vmem],
         out_specs=(vmem, vmem),
         scratch_shapes=[
             V((2 * BAND, BAND), f32), V((2 * BAND, BAND), f32), V((2 * BAND, BAND), f32),
             V((2, BAND, BAND), f32), V((2, BAND, BAND), f32), V((2, peers, BAND // rows_n, BAND), f32),
+            *[V((tall + 2 * HALO, wide), f32)] * 6,
             V((2, tall, wide), f32), V(kernel_spectra.shape, f32), V(kernel_spectra.shape, f32),
             V((kernels, 2, tall, GRID), f32), V((tall, GRID), f32), V((tall, GRID), f32),
             V((height, GRID), f32), V((height, GRID), f32),
@@ -325,7 +358,7 @@
         ],
         compiler_params=pltpu.CompilerParams(collective_id=0, has_side_effects=True, vmem_limit_bytes=60 * 2**20),
         name="resist_gradient",
-    )(mask_levels, target_image, root_rows, kernel_weights, kernel_spectra, m_hi, m_lo, u_hi, u_lo, t_hi, t_lo, r_all, p_fwd, p_bwd)
+    )(mask_levels, target_image, diffusion_index, diffusion_table, kernel_weights, kernel_spectra, m_hi, m_lo, u_hi, u_lo, t_hi, t_lo, r_all, p_fwd, p_bwd)
 
 
 def solution(mesh):

time: 88.6 us -> 85.4 us (0.964)
  local copies, waits for them, and re-layouts: 4.85 us -> 3.37 us
  Pallas kernels: 82.1 us -> 81.2 us
    pallas_call x1, Pallas kernels: 82.1 us -> 81.2 us  [body(): pl.pallas_call(lambda *refs: kernel(rows_n, *refs), out_shape=(jax.ShapeD...]
where the time goes in v3:
time: 85.4 us; the launch traced here: 85.3 us
  Pallas kernels  81.2 us (95%)
  local copies, waits for them, and re-layouts  3.37 us (4%)
    pallas_call x1, Pallas kernels, body(): pl.pallas_call(lambda *refs: kernel(rows_n, *refs), out_shape=(jax.ShapeD...  81.2 us
    unnamed x4, local copies, waits for them, and re-layouts  3.37 us

profile of v3, /device:TPU:0, one launch (start us, length us, event | category | flops | bytes accessed | tf_op | source)
XLA Modules:
  0.0 85.3 jit_solution(1476087840772982988)
XLA Ops:
  0.6 81.2 %resist_gradient.1 = (f32[256,1024]{1,0:T(8,128)}, f32[256,1024]{1,0:T(8,128)}) custom-call(f32[256,1024]{1,0:T(8,128)} %refs_0_.1, f32[256,1024]{1,0:T(8,128)} %refs_1_.1, s32[8,32]{1,0:T(8,128)} %refs_2_.1, f32[8]{0:T(128)} %refs_3_.1, f32[8]{0:T(128)} %refs_4_.1, f32[2,8,256,256]{3,2,1,0:T(8,128)} %refs_5_.1, bf16[2048,512]{1,0:T(8,128)(2,1)} %constant.18.clone.refs_6_, ...), custom_call_target="tpu_custom_call" | custom-call | tf_op jit(solution)/shard_map/resist_gradient/pallas_call | solution.py:342
  81.9 0.0 copy-start
  81.9 2.4 %copy.19 = f32[256,1024]{1,0:T(8,128)} copy(f32[256,1024]{1,0:T(8,128)} %get-tuple-element.4) | data formatting | bytes 2097152
  84.3 0.0 copy-done
  84.3 1.0 %copy.20 = f32[256,1024]{1,0:T(8,128)} copy(f32[256,1024]{1,0:T(8,128)S(1)} %copy-done) | data formatting | bytes 2097152
Async XLA Ops:
  81.9 2.4 %copy-start = (f32[256,1024]{1,0:T(8,128)S(1)}, f32[256,1024]{1,0:T(8,128)}, u32[]{:S(2)}) copy-start(f32[256,1024]{1,0:T(8,128)} %get-tuple-element.5) | copy-start | bytes 3145732

commit v4 on v3

--- a/solution.py
+++ b/solution.py
@@ -14,6 +14,7 @@
 GRID = 2 * BAND
 HALO = 2 * STEPS
 LANES = 128
+REAL = BAND + LANES
 steepness = 8.0
 threshold = 0.5
 MESH = pl.DeviceIdType.MESH
@@ -24,9 +25,22 @@
 
 def mask_table():
     n = np.arange(HALF)
-    f = np.concatenate([n, -(n + 1)])
-    angle = 2 * np.pi / PIXELS * ((f[:, None] * np.arange(PIXELS)[None, :]) % PIXELS)
-    return np.cos(angle), np.sin(angle)
+    pixel = np.arange(PIXELS)[:, None]
+    angle = lambda f: 2 * np.pi / PIXELS * ((f[None, :] * pixel) % PIXELS)
+    last = np.cos(angle(np.full(1, HALF)))
+    return np.concatenate([np.cos(angle(n)), np.sin(angle(np.where(n == 0, HALF, n))), last, np.zeros((PIXELS, LANES - 1))], 1)
+
+
+def unfold_matrix():
+    m = np.zeros((2 * BAND, REAL))
+    n = np.arange(HALF)
+    m[n, n] = 1.0
+    m[HALF + n[:-1], n[1:]] = 1.0
+    m[BAND - 1, BAND] = 1.0
+    m[BAND + n[1:], HALF + n[1:]] = 1.0
+    m[BAND + HALF + n[:-1], HALF + n[1:]] = -1.0
+    m[2 * BAND - 1, HALF] = -1.0
+    return jnp.asarray(m.astype(jnp.bfloat16))
 
 
 def half_table(positions):
@@ -107,11 +121,29 @@
     return jnp.concatenate([pad, x[height + HALO :], x[: height + HALO], pad], 0)
 
 
-def kernel(rows_n, mask, target, levels, level_values, weights, spectra, m_hi, m_lo, u_hi, u_lo, t_hi, t_lo, r_all, p_fwd, p_bwd,
+def pack(z, main, extra):
+    main[pl.ds(0, BAND)] = z[:BAND, :LANES]
+    main[pl.ds(BAND, BAND)] = z[:BAND, LANES:BAND]
+    flipped = z[:, BAND:].T
+    for n in range(3):
+        extra[n : n + 1, :] = z[BAND : BAND + 1, n * LANES : (n + 1) * LANES]
+        extra[3 + n : 4 + n, :] = flipped[0:1, n * LANES : (n + 1) * LANES]
+    extra[6:8, :] = jnp.zeros((2, LANES), jnp.float32)
+
+
+def unpack(main, extra):
+    beside = jnp.concatenate([extra[3:4], extra[4:5]], 1)
+    below = jnp.concatenate([extra[0:1], extra[1:2], extra[2:3]], 1)
+    top = lambda x: jnp.where(lax.broadcasted_iota(jnp.int32, (LANES, x.shape[1]), 0) == 0, jnp.broadcast_to(x, (LANES, x.shape[1])), 0.0)
+    upper = jnp.concatenate([main[pl.ds(0, BAND)], main[pl.ds(BAND, BAND)], top(beside).T], 1)
+    return jnp.concatenate([upper, top(below)], 0)
+
+
+def kernel(rows_n, mask, target, levels, level_values, weights, spectra, m_hi, m_lo, u_hi, u_lo, t_hi, t_lo, r_all, p_fwd, p_bwd, unfold,
            gradient, resist_out,
-           spec, full1, full2, pair_in, part, rs_in, ping, pong, c_up, c_down, c_left, c_right, both, h_in, h, fields, power, power_in, grid, grid_in,
+           spec, main, full1, full2, ext, ext_in, ext_part, ext_rows, pair_in, part, rs_in, ping, pong, c_up, c_down, c_left, c_right, both, h_in, h, fields, power, power_in, grid, grid_in,
            row_hi, row_lo, col_hi, col_lo, ut_hi, ut_lo, r_buf, transmit,
-           local_sem, pair_send, pair_recv, rs_send, rs_recv, ag_send, ag_recv):
+           local_sem, pair_send, pair_recv, rs_send, rs_recv, ag_send, ag_recv, ext_send, ext_recv):
     height, breadth = mask.shape
     tall, wide = both.shape[1:]
     kernels = h.shape[1]
@@ -177,14 +209,22 @@
     def allreduce(at, src, full, beside_pair=None, beside_scatter=None, beside_gather=None):
         swap = to_pair(src.at[pl.ds(partner * BAND, BAND)], pair_in.at[at], 1 + 2 * at)
         swap.start()
+        ext_swap = to_pair(ext.at[at], ext_in.at[at], 7 + at)
+        ext_swap.start()
         if beside_pair is not None:
             beside_pair()
         swap.wait()
+        ext_swap.wait()
+        ext_part[at] = ext[at] + ext_in[at]
         part[at] = src[pl.ds(col * BAND, BAND)] + pair_in[at]
         copies = []
         for o in range(1, rows_n):
             peer = lax.rem(row + o, rows_n)
             copies.append(to_row(part.at[at, pl.ds(peer * chunk, chunk)], rs_in.at[at, o - 1], peer, rs_send.at[at], rs_recv.at[at], o - 1))
+            copies[-1].start()
+        for o in range(1, rows_n):
+            peer = lax.rem(row + o, rows_n)
+            copies.append(to_row(ext_part.at[at], ext_rows.at[at, o - 1], peer, ext_send.at[at], ext_recv.at[at], o - 1))
             copies[-1].start()
         if beside_scatter is not None:
             beside_scatter()
@@ -207,7 +247,11 @@
         half = pl.ds(col * BAND, BAND)
         swap = to_pair(full.at[half], full.at[half], 2 + 2 * at)
         swap.start()
+        extra = ext_part[at]
+        for o in range(1, rows_n):
+            extra = extra + ext_rows[at, o - 1]
         swap.wait()
+        return unpack(full, extra)
 
     scale = 1.0 / (PIXELS * BAND)
     transmit[...] = jnp.tanh(mask[...])
@@ -217,8 +261,7 @@
     row_tab = (row_hi[...], row_lo[...])
     halfway = dot3(split(transmit[...]), col_tab)
     prod = dot3(row_tab, split(halfway), TN)
-    spec[pl.ds(0, BAND)] = (prod[:BAND, :BAND] - prod[BAND:, BAND:]) * scale
-    spec[pl.ds(BAND, BAND)] = -(prod[BAND:, :BAND] + prod[:BAND, BAND:]) * scale
+    pack(prod, main, ext.at[0])
 
     def fold(first, count):
         def step(k, _):
@@ -240,7 +283,13 @@
         for copy in local[4:]:
             copy.wait()
 
-    allreduce(0, spec, full1, beside_pair, lambda: fold(0, kernels // 2), lambda: fold(kernels // 2, kernels - kernels // 2))
+    real = allreduce(0, main, full1, beside_pair, lambda: fold(0, kernels // 2), lambda: fold(kernels // 2, kernels - kernels // 2))
+
+    real = split(real)
+    half_way = split(dot(unfold[...], real[0], NN) + dot(unfold[...], real[1], NN))
+    prod = dot(half_way[0], unfold[...], NT) + dot(half_way[1], unfold[...], NT)
+    spec[pl.ds(0, BAND)] = (prod[:BAND, :BAND] - prod[BAND:, BAND:]) * scale
+    spec[pl.ds(BAND, BAND)] = -(prod[BAND:, :BAND] + prod[:BAND, BAND:]) * scale
 
     t_tab = (t_hi[...], t_lo[...])
     r_tab = split(r_buf[...])
@@ -248,7 +297,7 @@
 
     def forward(k, _):
         h_re, h_im = h[0, k], h[1, k]
-        s_re, s_im = full1[pl.ds(0, BAND)], full1[pl.ds(BAND, BAND)]
+        s_re, s_im = spec[pl.ds(0, BAND)], spec[pl.ds(BAND, BAND)]
         ee_r, eo_r, oe_r, oo_r = quads(h_re * s_re - h_im * s_im)
         ee_i, eo_i, oe_i, oo_i = quads(h_re * s_im + h_im * s_re)
         square = 0.0
@@ -315,10 +364,12 @@
         return 0
 
     lax.fori_loop(0, kernels, backward, 0, unroll=2)
-    allreduce(1, spec, full2)
-    ds_re, ds_im = full2[pl.ds(0, BAND)] * scale, full2[pl.ds(BAND, BAND)] * scale
-    block = join(ds_re, -ds_im, -ds_im, -ds_re)
-    grad = dot3(split(dot3(row_tab, split(block))), col_tab, NT)
+    ds_re, ds_im = spec[pl.ds(0, BAND)] * scale, spec[pl.ds(BAND, BAND)] * scale
+    block = split(join(ds_re, -ds_im, -ds_im, -ds_re))
+    half_way = split(dot(block[0], unfold[...], NN) + dot(block[1], unfold[...], NN))
+    pack(dot(unfold[...], half_way[0], TN) + dot(unfold[...], half_way[1], TN), main, ext.at[1])
+    real = allreduce(1, main, full2)
+    grad = dot3(split(dot3(row_tab, split(real))), col_tab, NT)
     gradient[...] = grad * (1.0 - transmit[...] * transmit[...])
 
 
@@ -328,8 +379,7 @@
     assert cols_n == 2
     tall, wide = height + 2 * HALO, breadth + LANES
     kernels = kernel_weights.shape[0]
-    ct, st = mask_table()
-    m_hi, m_lo = halves(np.concatenate([ct.T, st.T], 1))
+    m_hi, m_lo = halves(mask_table())
     u_hi, u_lo = halves(interpolation_table().T)
     t_hi, t_lo = halves(half_table(np.arange(GRID) * (PIXELS // GRID)))
     r_all = jnp.asarray(half_table(np.arange(-HALO, PIXELS + HALO)).T.astype(np.float32))
@@ -342,23 +392,24 @@
     return pl.pallas_call(
         lambda *refs: kernel(rows_n, *refs),
         out_shape=(jax.ShapeDtypeStruct((height, breadth), f32),) * 2,
-        in_specs=[vmem, vmem, vmem, smem, smem, hbm, hbm, hbm, hbm, hbm, vmem, vmem, hbm, vmem, vmem],
+        in_specs=[vmem, vmem, vmem, smem, smem, hbm, hbm, hbm, hbm, hbm, vmem, vmem, hbm, vmem, vmem, vmem],
         out_specs=(vmem, vmem),
         scratch_shapes=[
-            V((2 * BAND, BAND), f32), V((2 * BAND, BAND), f32), V((2 * BAND, BAND), f32),
-            V((2, BAND, BAND), f32), V((2, BAND, BAND), f32), V((2, peers, BAND // rows_n, BAND), f32),
+            V((2 * BAND, BAND), f32), *[V((2 * BAND, LANES), f32)] * 3,
+            *[V((2, 8, LANES), f32)] * 3, V((2, peers, 8, LANES), f32),
+            V((2, BAND, LANES), f32), V((2, BAND, LANES), f32), V((2, peers, BAND // rows_n, LANES), f32),
             *[V((tall + 2 * HALO, wide), f32)] * 6,
             V((2, tall, wide), f32), V(kernel_spectra.shape, f32), V(kernel_spectra.shape, f32),
             V((kernels, 2, tall, GRID), f32), V((tall, GRID), f32), V((tall, GRID), f32),
             V((height, GRID), f32), V((height, GRID), f32),
-            V((height, 2 * BAND), bf16), V((height, 2 * BAND), bf16),
-            V((breadth, 2 * BAND), bf16), V((breadth, 2 * BAND), bf16),
+            V((height, REAL), bf16), V((height, REAL), bf16),
+            V((breadth, REAL), bf16), V((breadth, REAL), bf16),
             V((GRID, wide), bf16), V((GRID, wide), bf16), V((tall, BAND), f32), V((height, breadth), f32),
-            D((11,)), D((7,)), D((7,)), D((3, peers)), D((3, peers)), D((2, peers)), D((2, peers)),
+            D((11,)), D((9,)), D((9,)), D((3, peers)), D((3, peers)), *[D((2, peers))] * 4,
         ],
         compiler_params=pltpu.CompilerParams(collective_id=0, has_side_effects=True, vmem_limit_bytes=60 * 2**20),
         name="resist_gradient",
-    )(mask_levels, target_image, diffusion_index, diffusion_table, kernel_weights, kernel_spectra, m_hi, m_lo, u_hi, u_lo, t_hi, t_lo, r_all, p_fwd, p_bwd)
+    )(mask_levels, target_image, diffusion_index, diffusion_table, kernel_weights, kernel_spectra, m_hi, m_lo, u_hi, u_lo, t_hi, t_lo, r_all, p_fwd, p_bwd, unfold_matrix())
 
 
 def solution(mesh):

time: 85.4 us -> 81.9 us (0.959)
  Pallas kernels: 81.2 us -> 77.7 us
    pallas_call x1, Pallas kernels: 81.2 us -> 77.7 us  [body(): pl.pallas_call(lambda *refs: kernel(rows_n, *refs), out_shape=(jax.ShapeD...]
where the time goes in v4:
time: 81.9 us; the launch traced here: 81.7 us
  Pallas kernels  77.7 us (95%)
  local copies, waits for them, and re-layouts  3.37 us (4%)
    pallas_call x1, Pallas kernels, body(): pl.pallas_call(lambda *refs: kernel(rows_n, *refs), out_shape=(jax.ShapeD...  77.7 us
    unnamed x4, local copies, waits for them, and re-layouts  3.37 us

profile of v4, /device:TPU:0, one launch (start us, length us, event | category | flops | bytes accessed | tf_op | source)
XLA Modules:
  0.0 81.7 jit_solution(5203599682455894754)
XLA Ops:
  0.6 77.7 %resist_gradient.1 = (f32[256,1024]{1,0:T(8,128)}, f32[256,1024]{1,0:T(8,128)}) custom-call(f32[256,1024]{1,0:T(8,128)} %refs_0_.1, f32[256,1024]{1,0:T(8,128)} %refs_1_.1, s32[8,32]{1,0:T(8,128)} %refs_2_.1, f32[8]{0:T(128)} %refs_3_.1, f32[8]{0:T(128)} %refs_4_.1, f32[2,8,256,256]{3,2,1,0:T(8,128)} %refs_5_.1, bf16[2048,384]{1,0:T(8,128)(2,1)} %constant.20.clone.refs_6_, ...), custom_call_target="tpu_custom_call" | custom-call | tf_op jit(solution)/shard_map/resist_gradient/pallas_call | solution.py:392
  78.4 0.0 copy-start
  78.4 2.4 %copy.20 = f32[256,1024]{1,0:T(8,128)} copy(f32[256,1024]{1,0:T(8,128)} %get-tuple-element.4) | data formatting | bytes 2097152
  80.8 0.0 copy-done
  80.8 1.0 %copy.21 = f32[256,1024]{1,0:T(8,128)} copy(f32[256,1024]{1,0:T(8,128)S(1)} %copy-done) | data formatting | bytes 2097152
Async XLA Ops:
  78.4 2.4 %copy-start = (f32[256,1024]{1,0:T(8,128)S(1)}, f32[256,1024]{1,0:T(8,128)}, u32[]{:S(2)}) copy-start(f32[256,1024]{1,0:T(8,128)} %get-tuple-element.5) | copy-start | bytes 3145732
